TPU v7x, 512 devices: a whole 4x8x8 slice. The times are simulated.
512 devices in a mesh: ctx: 64 (over z_lo, y, core), head: 8 (over z_hi, x).
Axes of the slice: x: 4, y: 8, z: 8 (z_hi: 2, z_lo: 4; z = z_hi * 4 + z_lo), core: 2. Of those that a mesh axis runs over, the one named last changes fastest.
Arguments:
- q_attn: bfloat16 [128, 128, 576], P('ctx', 'head'), may hold values from -6 to 6
- latent: bfloat16 [65536, 576], P('ctx'), may hold values from -8 to 8
- lse_saved: float32 [128, 128], P('ctx', 'head'), may hold values from -2 to 2
- q_index: bfloat16 [128, 64, 128], P('ctx', 'head'), may hold values from -10 to 10
- k_index: bfloat16 [65536, 128], P('ctx'), may hold values from -6 to 6
- head_weight: float32 [128, 64], P('ctx', 'head'), may hold values from -1 to 1
Outputs:
- grad_query: float32 [128, 64, 128], P('ctx', 'head')
- grad_weight: float32 [128, 64], P('ctx', 'head')
- grad_key: float32 [65536, 128], P('ctx')
All inputs are finite; a program needn't handle non-finite values.
Results may differ from a plain program's by a relative error of at most 0.0105.
Values may be sent and summed in bfloat16 or wider, within the bound.
A program may use at most 64 MiB of HBM per device.

v0:
```python
import math

import jax
import jax.numpy as jnp
from jax import lax
from jax.sharding import PartitionSpec as P


def contract(left, right):
    return lax.dot_general(
        left, right, (((1,), (1,)), ((), ())), preferred_element_type=jnp.float32
    )


def residual_ctx(target_raw, index_score, factor):
    total_mass = jnp.sum(target_raw, axis=1)
    peak_value = jnp.max(index_score, axis=1)
    peak_value = lax.pmax(peak_value, "ctx")
    expo_terms = jnp.exp(index_score - peak_value[:, None])
    total_mass, exp_total = lax.psum((total_mass, jnp.sum(expo_terms, axis=1)), "ctx")
    return (factor * (expo_terms / exp_total[:, None] - target_raw / total_mass[:, None])).astype(
        jnp.bfloat16
    )


def body(q_attn, latent, lse_saved, q_index, k_index, head_weight):
    query_all, index_all = (
        lax.all_gather(q_attn, "ctx", axis=0, tiled=True),
        lax.all_gather(q_index, "ctx", axis=0, tiled=True),
    )
    lse_all, weight_all = (
        lax.all_gather(lse_saved, "ctx", axis=0, tiled=True),
        lax.all_gather(head_weight, "ctx", axis=0, tiled=True),
    )
    row_count = query_all.shape[0]
    head_count = query_all.shape[1]
    key_count = latent.shape[0]
    index_heads = index_all.shape[1]
    index_dim = index_all.shape[2]
    att_scale = latent.shape[1] ** (-0.5)
    factor = key_count * lax.axis_size("ctx") / 32.0
    group = math.gcd(head_count, 4)
    target_raw = jnp.zeros((row_count, key_count), jnp.float32)
    for block_index in range(head_count // group):
        lower = block_index * group
        queries_block = query_all[:, lower : lower + group, :].reshape(
            row_count * group, latent.shape[1]
        )
        scores = contract(queries_block, latent).reshape(row_count, group, key_count) * att_scale
        target_raw = target_raw + jnp.sum(
            jnp.exp(scores - lse_all[:, lower : lower + group, None]), axis=1
        )
    index_flat = index_all.reshape(row_count * index_heads, index_dim)
    index_raw = contract(index_flat, k_index).reshape(row_count, index_heads, key_count)
    index_relu = jnp.maximum(index_raw, 0.0)
    index_score = jnp.sum(weight_all[:, :, None] * index_relu, axis=1)
    target_raw = lax.psum(target_raw, "head")
    index_score = lax.psum(index_score, "head")
    grad_scores = residual_ctx(target_raw, index_score, factor)
    positive = index_raw > 0
    grad_f32 = grad_scores.astype(jnp.float32)[:, None, :]
    weight_part = jnp.sum(grad_f32 * index_relu, axis=2)
    masked = jnp.where(positive, grad_scores[:, None, :], jnp.zeros((), jnp.bfloat16))
    masked = masked.reshape(row_count * index_heads, key_count)
    query_part = jnp.dot(masked, k_index, preferred_element_type=jnp.float32).reshape(
        row_count, index_heads, index_dim
    )
    coeffs = jnp.where(positive, grad_f32 * weight_all[:, :, None], 0.0).astype(jnp.bfloat16)
    coeffs = coeffs.reshape(row_count * index_heads, key_count)
    key_part = lax.dot_general(
        coeffs, index_flat, (((0,), (0,)), ((), ())), preferred_element_type=jnp.float32
    )
    query_sum, grad_weight = (
        lax.psum_scatter(query_part, "ctx", scatter_dimension=0, tiled=True),
        lax.psum_scatter(weight_part, "ctx", scatter_dimension=0, tiled=True),
    )
    grad_key = lax.psum(key_part, "head")
    return (head_weight[:, :, None] * query_sum, grad_weight, grad_key)


def solution(mesh):
    return jax.shard_map(
        body,
        mesh=mesh,
        in_specs=(
            P("ctx", "head", None),
            P("ctx", None),
            P("ctx", "head"),
            P("ctx", "head", None),
            P("ctx", None),
            P("ctx", "head"),
        ),
        out_specs=(P("ctx", "head", None), P("ctx", "head"), P("ctx", None)),
        check_vma=False,
    )
```

profile of v0, /device:TPU:1, one launch (start us, length us, event | category | flops | bytes accessed | tf_op | source)
XLA Modules:
  0.0 1030.8 jit_solution(7292241986254674756)
XLA Ops:
  7.2 0.0 copy-start
  7.2 0.0 all-gather.4.cloned.1.call-start
  7.2 0.7 all-gather.4.cloned.1.call-update
  7.9 0.0 all-reduce.8.cloned.1.call-start
  8.0 84.2 %all-gather.1 = f32[64,2,16]{2,1,0:T(2,128)S(1)} all-gather(f32[1,2,16]{2,1,0:T(2,128)} %bitcast.26), channel_id=1, replica_groups=mesh['ctx'=64,'head'=8] {'ctx'}, dimensions={0}, use_global_device_ids=true | all-gather | bytes 8320 | tf_op jit(solution)/shard_map/all_gather | solution.py:32
  92.1 0.1 fusion.36
  92.2 0.1 copy.41
  92.3 0.1 copy.39
  92.4 0.1 copy.37
  92.5 0.1 copy.35
  92.5 74.3 %all-gather = f32[64,2,8]{2,1,0:T(2,128)S(1)} all-gather(f32[1,2,8]{2,1,0:T(2,128)} %bitcast.25), channel_id=1, replica_groups=mesh['ctx'=64,'head'=8] {'ctx'}, dimensions={0}, use_global_device_ids=true | all-gather | bytes 4160 | tf_op jit(solution)/shard_map/all_gather | solution.py:33
  166.8 76.2 %all_gather.12 = bf16[128,8,128]{2,1,0:T(8,128)(2,1)S(1)} all-gather(bf16[2,8,128]{2,1,0:T(8,128)(2,1)} %param.9), channel_id=1, replica_groups=mesh['ctx'=64,'head'=8] {'ctx'}, dimensions={0}, use_global_device_ids=true | all-gather | bytes 266240 | tf_op jit(solution)/shard_map/all_gather | solution.py:29
  243.1 4.5 multiply_reduce_fusion.1
  247.5 0.0 all-gather.4.cloned.1.call-done
  247.5 3.5 fusion.35
  251.1 0.0 copy-done
  251.1 1.1 exponential_reduce_fusion
  252.2 1.1 exponential_reduce_fusion.1
  253.2 1.1 exponential_reduce_fusion.2
  254.3 1.1 exponential_reduce_fusion.3
  255.4 0.9 add_add_fusion
  256.3 0.0 all-reduce.8.cloned.1.call-update
  256.4 0.0 reduce-scatter.2.cloned.1.call-start
  256.4 2.8 fusion.15
  259.2 0.0 copy-start.1
  259.2 107.0 %all-reduce.8.cloned.1.call-done = (f32[128,1024]{1,0:T(8,128)}, f32[128,1024]{1,0:T(8,128)}) async-done(((f32[128,1024]{1,0:T(8,128)}, f32[128,1024]{1,0:T(8,128)}), (f32[128,1024]{1,0:T(8,128)}, f32[128,1024]{1,0:T(8,128)})) %all-reduce.8.cloned.1.call-update) | async-done | bytes 1048592 | tf_op jit(solution)/shard_map/psum | solution.py:57
  366.2 1.2 reduce_max.9
  367.3 139.5 %pmax.7 = f32[128]{0:T(128)S(1)} all-reduce(f32[128]{0:T(128)S(1)} %reduce_max.9), channel_id=1, replica_groups=mesh['ctx'=64,'head'=8] {'ctx'}, use_global_device_ids=true, to_apply=%region_3.0 | all-reduce | flops 128 | bytes 1024 | tf_op jit(solution)/shard_map/pmax | solution.py:18
  506.9 1.3 fusion.24
  508.2 1.2 reduce_sum.78
  509.3 133.5 %all-reduce.1 = (f32[128]{0:T(128)S(1)}, f32[128]{0:T(128)S(1)}) all-reduce(f32[128]{0:T(128)S(1)} %reduce_sum.78, f32[128]{0:T(128)S(1)} %fusion.24), channel_id=1, replica_groups=mesh['ctx'=64,'head'=8] {'ctx'}, use_global_device_ids=true, to_apply=%region_12.0 | all-reduce | flops 256 | bytes 2048 | tf_op jit(solution)/shard_map/psum | solution.py:20
  642.8 1.4 fusion.34
  644.2 0.0 copy-done.1
  644.2 0.7 fusion.3
  644.9 1.1 copy.29
  646.0 0.0 reduce-scatter.2.cloned.1.call-update
  646.0 0.0 all-reduce.6.cloned.1.call-start
  646.1 1.3 dynamic-slice
  648.0 1.9 fusion.8
  649.9 0.0 all-reduce.6.cloned.1.call-update
  650.0 0.0 copy-start.2
  650.0 2.8 multiply_reduce_fusion
  652.8 0.1 copy.30
  652.9 259.3 %all-reduce = f32[128,8]{1,0:T(8,128)S(1)} all-reduce(f32[128,8]{1,0:T(8,128)S(1)} %copy.30), channel_id=3, replica_groups=mesh['ctx'=64,'head'=8] {'ctx'}, use_global_device_ids=true, to_apply=%region_15.16.clone | all-reduce | flops 1024 | bytes 8192
  912.2 0.6 constant_dynamic-slice_fusion
  912.7 0.0 reduce-scatter.2.cloned.1.call-done
  912.7 0.0 copy-done.2
  912.8 1.4 broadcast_multiply_fusion
  914.1 108.3 %all-reduce.6.cloned.1.call-done = f32[1024,128]{1,0:T(8,128)} async-done(((f32[1024,128]{1,0:T(8,128)}), f32[1024,128]{1,0:T(8,128)}) %all-reduce.6.cloned.1.call-update) | async-done | bytes 524304 | tf_op jit(solution)/shard_map/psum | solution.py:77
  1022.4 1.9 copy.59
  (1 shorter events, 0.0 us)
Async XLA Ops:
  7.2 243.9 %copy-start = (bf16[1024,576]{0,1:T(8,128)(2,1)S(1)}, bf16[1024,576]{0,1:T(8,128)(2,1)}, u32[]{:S(2)}) copy-start(bf16[1024,576]{0,1:T(8,128)(2,1)} %param.7) | copy-start | bytes 3538948
  7.2 240.4 %all-gather.4.cloned.1.call-start = ((), (), s32[]{:S(2)}) async-start(), calls=%async_computation.1 | async-start | bytes 2662400 | tf_op jit(solution)/shard_map/all_gather | solution.py:28
  7.9 358.3 %all-reduce.8.cloned.1.call-start = ((), (), s32[]{:S(2)}) async-start(), calls=%async_computation.4 | async-start | bytes 2097152 | tf_op jit(solution)/shard_map/psum | solution.py:57
  256.4 656.4 %reduce-scatter.2.cloned.1.call-start = ((), (), s32[]{:S(2)}) async-start(), calls=%async_computation.2 | async-start | bytes 532480 | tf_op jit(solution)/shard_map/reduce_scatter | solution.py:74
  259.2 385.0 %copy-start.1 = (bf16[1024,128]{1,0:T(8,128)(2,1)S(1)}, bf16[1024,128]{1,0:T(8,128)(2,1)}, u32[]{:S(2)}) copy-start(bf16[1024,128]{1,0:T(8,128)(2,1)} %param.10) | copy-start | bytes 786436
  646.0 376.3 %all-reduce.6.cloned.1.call-start = ((), (), s32[]{:S(2)}) async-start(), calls=%async_computation.3 | async-start | bytes 1048576 | tf_op jit(solution)/shard_map/psum | solution.py:77
  650.0 262.8 %copy-start.2 = (f32[2,8]{1,0:T(2,128)S(1)}, f32[2,8]{1,0:T(2,128)}, u32[]{:S(2)}) copy-start(f32[2,8]{1,0:T(2,128)} %param.11) | copy-start | bytes 196
Sparse Core Ops, SparseCore 0:
  10.2 125.3 all-gather.3
  256.5 109.6 all-reduce.7
  646.2 265.4 reduce-scatter.1
  914.7 107.6 all-reduce.5
where the time goes:
time: 1040 us; the launch traced here: 1030 us
  blocking collectives  767 us (74%)
  waiting for transfers between devices  216 us (21%)
  between operations  14.5 us (1%)
  other arithmetic  12.8 us (1%)
  matrix products  11.4 us (1%)
    unnamed x1, blocking collectives  259 us
    pmax x1, blocking collectives, residual_ctx(): peak_value = lax.pmax(peak_value, 'ctx')  140 us
    psum x1, blocking collectives, residual_ctx(): lax.psum((total_mass, jnp.sum(expo_terms, axis=1)), 'ctx')  133 us
    psum x1, waiting for transfers between devices, body(): grad_key = lax.psum(key_part, 'head')  108 us
    psum x1, waiting for transfers between devices, body(): target_raw = lax.psum(target_raw, 'head')  107 us
    all_gather x1, blocking collectives, body(): lax.all_gather(lse_saved, 'ctx', axis=0, tiled=True)  84.2 us
    all_gather x1, blocking collectives, body(): lax.all_gather(q_index, 'ctx', axis=0, tiled=True)  76.2 us
    all_gather x1, blocking collectives, body(): lax.all_gather(head_weight, 'ctx', axis=0, tiled=True)  74.3 us
  transfers between devices with their start and end apart: 4, of which 2 were waited for; matrix products, arithmetic and copies ran while one was open for 2% of the time, Pallas kernels for 0%

commit v1 on v0

v1 whole, which is shorter than its diff:
```python
import functools
import math

import jax
import jax.numpy as jnp
from jax import lax
from jax.experimental import pallas as pl
from jax.experimental.pallas import tpu as pltpu
from jax.sharding import PartitionSpec as P

MESH = pl.DeviceIdType.MESH
F32, BF16 = jnp.float32, jnp.bfloat16
DIMS = (4, 8, 2, 4)
NT = (((1,), (1,)), ((), ()))


def split3(v):
    hi = v.astype(BF16).astype(F32)
    mid = (v - hi).astype(BF16).astype(F32)
    return hi, mid, v - hi - mid


def column(row):
    n = row.shape[1]
    eye = lax.broadcasted_iota(jnp.int32, (n, n), 0) == lax.broadcasted_iota(jnp.int32, (n, n), 1)
    return jnp.sum(jnp.where(eye, row, 0.0), axis=1, keepdims=True)


def row_of(col):
    n = col.shape[0]
    eye = lax.broadcasted_iota(jnp.int32, (n, n), 0) == lax.broadcasted_iota(jnp.int32, (n, n), 1)
    return jnp.sum(jnp.where(eye, col, 0.0), axis=0, keepdims=True)


def kernel(
    dims, factor,
    q_ref, lat_ref, lse_ref, qi_ref, k_ref, w_ref,
    gq_ref, gw_ref, gk_ref,
    q_stage, i_stage, qbuf, ibuf, latbuf, kbuf, raw, wq, tacc, sacc, gbuf, masked,
    sy_buf, sz_buf, part, ry_buf, zsum, fq_buf,
    ck_own, ck_send, ck_recv, gx_sum, gx_send, gx_recv, gz_send, gz_recv, ga_buf,
    s_entry, r_entry, s_core, r_core, s_zq, s_zi, s_yp, s_ym, s_yi, r_q, r_i,
    s_sy, r_sy, s_sz, r_sz, s_ry, r_ry, s_fq, r_fq, s_gx, r_gx, s_gz, r_gz, s_ga, r_ga,
):
    NZ, NY, NZH, NX = dims
    ctx, head = lax.axis_index("ctx"), lax.axis_index("head")
    c = lax.rem(ctx, 2)
    y = lax.rem(lax.div(ctx, 2), NY)
    zl = lax.div(ctx, 2 * NY)
    x = lax.rem(head, NX)
    zh = lax.div(head, NX)
    rows, heads, width = q_ref.shape
    iheads, idim = qi_ref.shape[1:]
    nk = lat_ref.shape[0]
    wide = qbuf.shape[-1]
    R = NZ * rows
    K2 = 2 * nk
    base = wide - 128
    tail = width - base
    scale = width ** -0.5
    inv_scale = width ** 0.5
    log2e = math.log2(math.e)

    def ctx_of(zl_, y_, c_):
        return (zl_ * NY + y_) * 2 + c_

    def rcopy(src, dst, ssem, rsem, ctx_, head_):
        return pltpu.make_async_remote_copy(
            src_ref=src, dst_ref=dst, send_sem=ssem, recv_sem=rsem,
            device_id={"ctx": ctx_, "head": head_}, device_id_type=MESH,
        )

    def arrived(dst, rsem):
        pltpu.make_async_copy(dst, dst, rsem).wait()

    y_peers = [lax.rem(y + d, NY) for d in range(1, NY)]
    z_peers = [lax.rem(zl + d, NZ) for d in range(1, NZ)]
    x_peers = [lax.rem(x + d, NX) for d in range(1, NX)]
    fixed = head == y

    barrier = pltpu.get_barrier_semaphore()

    def greet(ctx_, head_):
        pl.semaphore_signal(barrier, inc=1, device_id={"ctx": ctx_, "head": head_}, device_id_type=MESH)

    greet(ctx_of(zl, y, 1 - c), head)
    for y_ in y_peers:
        greet(ctx_of(zl, y_, c), head)
    for z_ in z_peers:
        greet(ctx_of(z_, y, c), head)
        greet(ctx_of(z_, head, c), y)
    for x_ in x_peers:
        greet(ctx, zh * NX + x_)
    greet(ctx, (1 - zh) * NX + x)

    @pl.when(jnp.logical_not(fixed))
    def _():
        greet(ctx_of(zl, head, c), y)

    lane = lax.broadcasted_iota(jnp.int32, (heads, 128), 1)
    for r in range(rows):
        t3 = [v for v in split3(column(lse_ref[r : r + 1, :]))]
        w3 = [jnp.concatenate([v, jnp.zeros((heads - iheads, 1), F32)], axis=0)
              for v in split3(column(w_ref[r : r + 1, :]))]
        aug = jnp.zeros((heads, 128), F32)
        for n, v in enumerate(t3 + w3):
            aug = jnp.where(lane == tail + n, v, aug)
        q_stage[r * heads : (r + 1) * heads, :base] = q_ref[r, :, :base]
        last = jnp.concatenate([q_ref[r, :, base:].astype(F32), jnp.zeros((heads, 128 - tail), F32)], axis=1)
        q_stage[r * heads : (r + 1) * heads, base:] = (last + aug).astype(BF16)
    i_stage[...] = qi_ref[...].astype(F32).reshape(rows * iheads, idim).astype(BF16)
    latbuf[:nk, :base] = lat_ref[:, :base]
    klane = lax.broadcasted_iota(jnp.int32, (nk, 128 - tail), 1)
    kaug = jnp.where(klane < 3, -inv_scale, 0.0).astype(F32)
    latbuf[:nk, base:] = jnp.concatenate([lat_ref[:, base:].astype(F32), kaug], axis=1).astype(BF16)
    kbuf[:nk] = k_ref[...]

    pl.semaphore_wait(barrier, jnp.where(fixed, 1 + (NY - 1) + 2 * (NZ - 1) + (NX - 1) + 1,
                                         2 + (NY - 1) + 2 * (NZ - 1) + (NX - 1) + 1))

    @pl.when(jnp.logical_not(fixed))
    def _():
        rcopy(i_stage, ibuf.at[head, zl], s_entry.at[0], r_i.at[head, zl], ctx_of(zl, head, c), y).start()
        rcopy(q_stage, qbuf.at[head, zl], s_entry.at[1], r_q.at[head, zl], ctx_of(zl, head, c), y).start()

    @pl.when(fixed)
    def _():
        pltpu.make_async_copy(i_stage, ibuf.at[y, zl], r_i.at[y, zl]).start()
        pltpu.make_async_copy(q_stage, qbuf.at[y, zl], r_q.at[y, zl]).start()

    other = ctx_of(zl, y, 1 - c)
    k_copy = rcopy(kbuf.at[:nk], kbuf.at[nk:], s_core.at[0], r_core.at[0], other, head)
    lat_copy = rcopy(latbuf.at[:nk], latbuf.at[nk:], s_core.at[1], r_core.at[1], other, head)
    k_copy.start()
    lat_copy.start()

    tacc[...] = jnp.zeros_like(tacc)
    sacc[...] = jnp.zeros_like(sacc)

    sends = []
    up, down = lax.rem(y + 1, NY), lax.rem(y + NY - 1, NY)
    half_up = NY // 2
    half_down = NY - 1 - half_up

    def forward(y0, z0, step, plus, minus):
        if plus:
            cp = rcopy(qbuf.at[y0, z0], qbuf.at[y0, z0], s_yp.at[step, z0], r_q.at[y0, z0], ctx_of(zl, up, c), head)
            cp.start()
            sends.append(cp)
        if minus:
            cp = rcopy(qbuf.at[y0, z0], qbuf.at[y0, z0], s_ym.at[step, z0], r_q.at[y0, z0], ctx_of(zl, down, c), head)
            cp.start()
            sends.append(cp)

    arrived(ibuf.at[y, zl], r_i.at[y, zl])
    for n, z_ in enumerate(z_peers):
        cp = rcopy(ibuf.at[y, zl], ibuf.at[y, zl], s_zi.at[n], r_i.at[y, zl], ctx_of(z_, y, c), head)
        cp.start()
        sends.append(cp)
    arrived(qbuf.at[y, zl], r_q.at[y, zl])
    for n, z_ in enumerate(z_peers):
        cp = rcopy(qbuf.at[y, zl], qbuf.at[y, zl], s_zq.at[n], r_q.at[y, zl], ctx_of(z_, y, c), head)
        cp.start()
        sends.append(cp)
    forward(y, zl, 0, half_up > 0, half_down > 0)
    for z_ in z_peers:
        arrived(ibuf.at[y, z_], r_i.at[y, z_])
    for n, y_ in enumerate(y_peers):
        cp = rcopy(ibuf.at[y], ibuf.at[y], s_yi.at[n], r_yi(r_i, y), ctx_of(zl, y_, c), head)
        cp.start()
        sends.append(cp)
    for z_ in z_peers:
        arrived(qbuf.at[y, z_], r_q.at[y, z_])
        forward(y, z_, 0, half_up > 0, half_down > 0)

    CH = min(512, K2)

    def block(y0):
        q = qbuf[y0].reshape(R * heads, wide)
        qi = ibuf[y0].reshape(R * iheads, idim)
        aug = qbuf[y0, :, :, base:].astype(F32).reshape(R * heads, 128)
        ln = lax.broadcasted_iota(jnp.int32, aug.shape, 1)
        wide_col = jnp.sum(jnp.where((ln >= tail + 3) & (ln < tail + 6), aug, 0.0), axis=1, keepdims=True)
        wcol = wide_col.reshape(R, heads, 1)[:, :iheads, :]
        wq[y0] = (qi.astype(F32).reshape(R, iheads, idim) * wcol).reshape(R * iheads, idim).astype(BF16)

        @pl.loop(0, K2 // CH)
        def _(n):
            cols = pl.ds(pl.multiple_of(n * CH, CH), CH)
            s = lax.dot_general(q, latbuf[cols, :], NT, preferred_element_type=F32)
            e = jnp.exp2(s * (scale * log2e))
            tacc[:, :, cols] += jnp.sum(e.reshape(R, heads // 8, 8, CH), axis=1)
            rw = lax.dot_general(qi, kbuf[cols, :], NT, preferred_element_type=F32)
            raw[y0, :, cols] = rw
            sacc[:, :, cols] += wcol * jnp.maximum(rw, 0.0).reshape(R, iheads, CH)

    k_copy.wait_recv()
    lat_copy.wait_recv()
    block(y)
    for step in range(1, half_up + 1):
        yu = lax.rem(y + NY - step, NY)
        yd = lax.rem(y + step, NY)
        for n in range(NZ):
            z_ = lax.rem(zl + n, NZ)
            arrived(qbuf.at[yu, z_], r_q.at[yu, z_])
            forward(yu, z_, step, step < half_up, False)
            if step <= half_down:
                arrived(qbuf.at[yd, z_], r_q.at[yd, z_])
                forward(yd, z_, step, False, step < half_down)
        arrived(ibuf.at[yu], r_yi(r_i, yu))
        block(yu)
        if step <= half_down:
            arrived(ibuf.at[yd], r_yi(r_i, yd))
            block(yd)

    target = jnp.sum(tacc[...], axis=1)
    score = jnp.sum(sacc[...], axis=1)
    m = jnp.max(score, axis=1, keepdims=True)
    l = jnp.sum(jnp.exp(score - m), axis=1, keepdims=True)
    t = jnp.sum(target, axis=1, keepdims=True)
    sl = lax.broadcasted_iota(jnp.int32, (R, 128), 1)

    def exchange(buf, me, peers, where, ssem, rsem, m, l, t):
        buf[me] = jnp.where(sl == 0, m, jnp.where(sl == 1, l, t))
        for n, p in enumerate(peers):
            cp = rcopy(buf.at[me], buf.at[me], ssem.at[n], rsem.at[me], where(p), head)
            cp.start()
            sends.append(cp)
        for p in peers:
            arrived(buf.at[p], rsem.at[p])
        all_ = buf[...]
        mm = jnp.max(all_[:, :, 0:1], axis=0)
        ll = jnp.sum(all_[:, :, 1:2] * jnp.exp(all_[:, :, 0:1] - mm[None]), axis=0)
        tt = jnp.sum(all_[:, :, 2:3], axis=0)
        return mm, ll, tt

    m, l, t = exchange(sy_buf, y, y_peers, lambda p: ctx_of(zl, p, c), s_sy, r_sy, m, l, t)
    m, l, t = exchange(sz_buf, zl, z_peers, lambda p: ctx_of(p, y, c), s_sz, r_sz, m, l, t)
    grad = factor * (jnp.exp(score - m) / l - target / t)
    gbuf[...] = grad.astype(BF16).astype(F32)

    @pl.loop(0, NY)
    def _(y0):
        keep = raw[y0].reshape(R, iheads, K2) > 0
        g = jnp.where(keep, gbuf[...][:, None, :], 0.0)
        masked[y0] = g.reshape(R * iheads, K2).astype(BF16)

    mk = masked[...].reshape(NY * R * iheads, K2)
    wqt = wq[...].reshape(NY * R * iheads, idim).astype(F32).T.astype(BF16)
    gkt = jnp.dot(wqt, mk, preferred_element_type=F32)
    ck_send[...] = gkt[:, nk:].astype(BF16)
    ck_copy = rcopy(ck_send, ck_recv, s_core.at[2], r_core.at[2], other, head)
    ck_copy.start()
    ck_own[...] = gkt[:, :nk]
    part[...] = jnp.dot(mk, kbuf[...], preferred_element_type=F32).reshape(part.shape).astype(part.dtype)
    for n, y_ in enumerate(y_peers):
        cp = rcopy(part.at[y_], ry_buf.at[y], s_ry.at[n], r_ry.at[y], ctx_of(zl, y_, c), head)
        cp.start()
        sends.append(cp)

    ck_copy.wait_recv()
    nq = nk // NX
    for n in range(NX):
        v = ck_own[:, n * nq : (n + 1) * nq] + ck_recv[:, n * nq : (n + 1) * nq].astype(F32)
        gx_sum[n] = v
        gx_send[n] = v.astype(BF16)
    for n, x_ in enumerate(x_peers):
        cp = rcopy(gx_send.at[x_], gx_recv.at[x], s_gx.at[n], r_gx.at[x], ctx, zh * NX + x_)
        cp.start()
        sends.append(cp)

    total = part[y].astype(F32)
    for y_ in y_peers:
        arrived(ry_buf.at[y_], r_ry.at[y_])
        total = total + ry_buf[y_].astype(F32)
    zsum[...] = total.reshape(zsum.shape)

    for n in range(NZ):
        z_ = lax.rem(zl + n, NZ)
        if n == 0:
            @pl.when(jnp.logical_not(fixed))
            def _():
                rcopy(zsum.at[zl], fq_buf.at[zl], s_fq.at[0], r_fq.at[zl], ctx_of(zl, head, c), y).start()

            @pl.when(fixed)
            def _():
                pltpu.make_async_copy(zsum.at[zl], fq_buf.at[zl], r_fq.at[zl]).start()
        else:
            cp = rcopy(zsum.at[z_], fq_buf.at[zl], s_fq.at[n], r_fq.at[zl], ctx_of(z_, head, c), y)
            cp.start()
            sends.append(cp)

    gsum = gx_sum[x]
    for x_ in x_peers:
        arrived(gx_recv.at[x_], r_gx.at[x_])
        gsum = gsum + gx_recv[x_].astype(F32)
    gz_send[...] = gsum.astype(BF16)
    gz_copy = rcopy(gz_send, gz_recv, s_gz.at[0], r_gz.at[0], ctx, (1 - zh) * NX + x)
    gz_copy.start()
    gz_copy.wait_recv()
    gsum = gz_send[...].astype(F32) + gz_recv[...].astype(F32)
    ga_buf[x] = gsum.T.astype(BF16)
    for n, x_ in enumerate(x_peers):
        cp = rcopy(ga_buf.at[x], ga_buf.at[x], s_ga.at[n], r_ga.at[x], ctx, zh * NX + x_)
        cp.start()
        sends.append(cp)

    for n in range(NZ):
        z_ = lax.rem(zl + n, NZ)
        arrived(fq_buf.at[z_], r_fq.at[z_])
    qsum = jnp.sum(fq_buf[...], axis=0)
    for r in range(rows):
        own = qsum[r * iheads : (r + 1) * iheads]
        gq_ref[r] = own * column(w_ref[r : r + 1, :])
        gw_ref[r : r + 1, :] = row_of(jnp.sum(own * qi_ref[r].astype(F32), axis=1, keepdims=True))

    for x_ in x_peers:
        arrived(ga_buf.at[x_], r_ga.at[x_])
    gk_ref[...] = ga_buf[...].astype(F32).reshape(gk_ref.shape)

    for cp in sends:
        cp.wait_send()
    k_copy.wait_send()
    lat_copy.wait_send()
    ck_copy.wait_send()
    gz_copy.wait_send()

    @pl.when(jnp.logical_not(fixed))
    def _():
        rcopy(i_stage, ibuf.at[head, zl], s_entry.at[0], r_i.at[head, zl], ctx_of(zl, head, c), y).wait_send()
        rcopy(q_stage, qbuf.at[head, zl], s_entry.at[1], r_q.at[head, zl], ctx_of(zl, head, c), y).wait_send()
        rcopy(zsum.at[zl], fq_buf.at[zl], s_fq.at[0], r_fq.at[zl], ctx_of(zl, head, c), y).wait_send()


def r_yi(r_i, y0):
    return r_i.at[y0, r_i.shape[1] - 1]


def body(dims, keys, q_attn, latent, lse_saved, q_index, k_index, head_weight):
    NZ, NY, NZH, NX = dims
    rows, heads, width = q_attn.shape
    iheads, idim = q_index.shape[1:]
    nk = latent.shape[0]
    wide = -(-width // 128) * 128
    R = NZ * rows
    K2 = 2 * nk
    nq = nk // NX
    V, DMA = pltpu.VMEM, pltpu.SemaphoreType.DMA
    vm = pl.BlockSpec(memory_space=pltpu.VMEM)
    scratch = [
        V((rows * heads, wide), BF16), V((rows * iheads, idim), BF16),
        V((NY, NZ, rows * heads, wide), BF16), V((NY, NZ, rows * iheads, idim), BF16),
        V((K2, wide), BF16), V((K2, idim), BF16),
        V((NY, R * iheads, K2), F32), V((NY, R * iheads, idim), BF16),
        V((R, 8, K2), F32), V((R, iheads, K2), F32), V((R, K2), F32), V((NY, R * iheads, K2), BF16),
        V((NY, R, 128), F32), V((NZ, R, 128), F32),
        V((NY, R * iheads, idim), BF16), V((NY, R * iheads, idim), BF16),
        V((NZ, rows * iheads, idim), F32), V((NZ, rows * iheads, idim), F32),
        V((idim, nk), F32), V((idim, nk), BF16), V((idim, nk), BF16),
        V((NX, idim, nq), F32), V((NX, idim, nq), BF16), V((NX, idim, nq), BF16),
        V((idim, nq), BF16), V((idim, nq), BF16), V((NX, nq, idim), BF16),
        DMA((2,)), DMA((2,)), DMA((3,)), DMA((3,)), DMA((NZ,)), DMA((NZ,)),
        DMA((NY, NZ)), DMA((NY, NZ)), DMA((NY,)), DMA((NY, NZ)), DMA((NY, NZ + 1)),
        DMA((NY,)), DMA((NY,)), DMA((NZ,)), DMA((NZ,)), DMA((NY,)), DMA((NY,)), DMA((NZ,)), DMA((NZ,)),
        DMA((NX,)), DMA((NX,)), DMA((1,)), DMA((1,)), DMA((NX,)), DMA((NX,)),
    ]
    return pl.pallas_call(
        functools.partial(kernel, dims, keys / 32.0),
        out_shape=(
            jax.ShapeDtypeStruct((rows, iheads, idim), F32),
            jax.ShapeDtypeStruct((rows, iheads), F32),
            jax.ShapeDtypeStruct((nk, idim), F32),
        ),
        in_specs=[vm] * 6,
        out_specs=(vm, vm, vm),
        scratch_shapes=scratch,
        compiler_params=pltpu.CompilerParams(
            collective_id=0, has_side_effects=True, vmem_limit_bytes=48 * 1024 * 1024
        ),
        name="indexer_backward",
    )(q_attn, latent, lse_saved, q_index, k_index, head_weight)


def build(mesh, dims, keys):
    return jax.shard_map(
        functools.partial(body, dims, keys),
        mesh=mesh,
        in_specs=(
            P("ctx", "head", None),
            P("ctx", None),
            P("ctx", "head"),
            P("ctx", "head", None),
            P("ctx", None),
            P("ctx", "head"),
        ),
        out_specs=(P("ctx", "head", None), P("ctx", "head"), P("ctx", None)),
        check_vma=False,
    )


def solution(mesh):
    return build(mesh, DIMS, 65536)
```

time: 1040 us -> 85.6 us (0.08)
  blocking collectives: 767 us -> 0 us
  waiting for transfers between devices: 216 us -> 0 us
  Pallas kernels: 0 us -> 80.2 us
  between operations: 14.5 us -> 0.73 us
  other arithmetic: 12.8 us -> 0 us
  matrix products: 11.4 us -> 0 us
    unnamed x1 -> x0, blocking collectives: 259 us -> none
    all_gather x3 -> x0, blocking collectives: 235 us -> none  [the longest x1 84.2 us: body(): lax.all_gather(lse_saved, 'ctx', axis=0, tiled=True)]
    psum x2 -> x0, waiting for transfers between devices: 215 us -> none  [the longest x1 108 us: body(): grad_key = lax.psum(key_part, 'head')]
    pmax x1 -> x0, blocking collectives: 140 us -> none  [residual_ctx(): peak_value = lax.pmax(peak_value, 'ctx')]
    psum x1 -> x0, blocking collectives: 133 us -> none  [residual_ctx(): lax.psum((total_mass, jnp.sum(expo_terms, axis=1)), 'ctx')]
    pallas_call x0 -> x1, Pallas kernels: none -> 80.2 us  [body(): pl.pallas_call(functools.partial(kernel, dims, keys / 32.0), out_shape=(j...]
    dot_general x7 -> x0, matrix products: 11.4 us -> none  [the longest x5 8.76 us: contract(): lax.dot_general(left, right, (((1,), (1,)), ((), ())), preferred_element_...]
  transfers between devices with their start and end apart: 4 -> 0, of which waited for: 2 -> 0; matrix products, arithmetic and copies ran while one was open for 2% -> 0% of each run, Pallas kernels for 0% -> 0%
where the time goes in v1:
time: 85.6 us; the launch traced here: 84.6 us
  Pallas kernels  80.2 us (94%)
  local copies, waits for them, and re-layouts  3.7 us (4%)
    pallas_call x1, Pallas kernels, body(): pl.pallas_call(functools.partial(kernel, dims, keys / 32.0), out_shape=(j...  80.2 us
    unnamed x14, local copies, waits for them, and re-layouts  3.7 us

profile of v1, /device:TPU:1, one launch (start us, length us, event | category | flops | bytes accessed | tf_op | source)
XLA Modules:
  0.0 84.6 jit_solution(4217084043981688194)
XLA Ops:
  0.6 0.0 copy-start.4
  0.6 0.0 copy-start
  0.7 0.0 copy-start.2
  0.7 0.0 copy-start.3
  0.7 0.0 copy-start.1
  0.7 1.7 %copy.9.lat_ref = bf16[1024,576]{1,0:T(8,128)(2,1)S(1)} copy(bf16[1024,576]{0,1:T(8,128)(2,1)} %param.7) | data formatting | bytes 2359296 | tf_op args[1]
  2.4 0.0 copy-done.4
  2.4 0.0 copy-done
  2.4 0.0 copy-done.2
  2.4 0.0 copy-done.3
  2.4 0.0 copy-done.1
  2.5 80.2 %indexer_backward.1 = (f32[2,8,128]{2,1,0:T(8,128)S(1)}, f32[2,8]{1,0:T(2,128)S(1)}, f32[1024,128]{1,0:T(8,128)S(1)}) custom-call(bf16[2,16,576]{2,1,0:T(8,128)(2,1)S(1)} %copy-done.1, bf16[1024,576]{1,0:T(8,128)(2,1)S(1)} %copy.9.lat_ref, f32[2,16]{1,0:T(2,128)S(1)} %copy-done.3, bf16[2,8,128]{2,1,0:T(8,128)(2,1)S(1)} %copy-done.2, ...), custom_call_target="tpu_custom_call" | custom-call | tf_op jit(solution)/shard_map/indexer_backward/pallas_call | solution.py:367
  82.7 0.6 copy.13
  83.3 0.6 copy.14
  83.9 0.8 copy.15
Async XLA Ops:
  0.6 1.8 %copy-start.4 = (f32[2,8]{1,0:T(2,128)S(1)}, f32[2,8]{1,0:T(2,128)}, u32[]{:S(2)}) copy-start(f32[2,8]{1,0:T(2,128)} %w_ref.1) | copy-start | bytes 196
  0.6 1.8 %copy-start = (bf16[1024,128]{1,0:T(8,128)(2,1)S(1)}, bf16[1024,128]{1,0:T(8,128)(2,1)}, u32[]{:S(2)}) copy-start(bf16[1024,128]{1,0:T(8,128)(2,1)} %k_ref.1) | copy-start | bytes 786436
  0.7 1.8 %copy-start.2 = (bf16[2,8,128]{2,1,0:T(8,128)(2,1)S(1)}, bf16[2,8,128]{2,1,0:T(8,128)(2,1)}, u32[]{:S(2)}) copy-start(bf16[2,8,128]{2,1,0:T(8,128)(2,1)} %qi_ref.1) | copy-start | bytes 12292
  0.7 1.8 %copy-start.3 = (f32[2,16]{1,0:T(2,128)S(1)}, f32[2,16]{1,0:T(2,128)}, u32[]{:S(2)}) copy-start(f32[2,16]{1,0:T(2,128)} %lse_ref.1) | copy-start | bytes 388
  0.7 1.8 %copy-start.1 = (bf16[2,16,576]{2,1,0:T(8,128)(2,1)S(1)}, bf16[2,16,576]{2,1,0:T(8,128)(2,1)}, u32[]{:S(2)}) copy-start(bf16[2,16,576]{2,1,0:T(8,128)(2,1)} %q_ref.1) | copy-start | bytes 110596

commit v2 on v1

v2 whole, which is shorter than its diff:
```python
import functools
import math

import jax
import jax.numpy as jnp
from jax import lax
from jax.experimental import pallas as pl
from jax.experimental.pallas import tpu as pltpu
from jax.sharding import PartitionSpec as P

MESH = pl.DeviceIdType.MESH
F32, BF16 = jnp.float32, jnp.bfloat16
DIMS = (4, 8, 2, 4)
NT = (((1,), (1,)), ((), ()))


def split3(v):
    hi = v.astype(BF16).astype(F32)
    mid = (v - hi).astype(BF16).astype(F32)
    return hi, mid, v - hi - mid


def column(row):
    n = row.shape[1]
    eye = lax.broadcasted_iota(jnp.int32, (n, n), 0) == lax.broadcasted_iota(jnp.int32, (n, n), 1)
    return jnp.sum(jnp.where(eye, row, 0.0), axis=1, keepdims=True)


def row_of(col):
    n = col.shape[0]
    eye = lax.broadcasted_iota(jnp.int32, (n, n), 0) == lax.broadcasted_iota(jnp.int32, (n, n), 1)
    return jnp.sum(jnp.where(eye, col, 0.0), axis=0, keepdims=True)


def kernel(
    dims, factor,
    q_ref, lat_ref, lse_ref, qi_ref, k_ref, w_ref,
    gq_ref, gw_ref, gk_ref,
    q_stage, i_stage, qbuf, ientry, ibuf, latbuf, kbuf, raw, wq, tacc, sacc, gbuf, masked,
    sy_buf, sz_buf, part, ry_buf, zsum, fq_buf,
    ck_send, ck_recv, gx_sum, gx_send, gx_recv, gz_send, gz_recv, ga_buf,
    s_eq, s_ei, r_eq, r_ei, s_core, r_core, s_up, s_down, r_y,
    s_sy, r_sy, s_sz, r_sz, s_ry, r_ry, s_fq, r_fq, s_gx, r_gx, s_gz, r_gz, s_ga, r_ga,
):
    NZ, NY, NZH, NX = dims
    NH = NZH * NX
    ctx, head = lax.axis_index("ctx"), lax.axis_index("head")
    c = lax.rem(ctx, 2)
    y = lax.rem(lax.div(ctx, 2), NY)
    zl = lax.div(ctx, 2 * NY)
    x = lax.rem(head, NX)
    zh = lax.div(head, NX)
    rows, heads, width = q_ref.shape
    iheads, idim = qi_ref.shape[1:]
    nk = lat_ref.shape[1]
    wide = qbuf.shape[-1]
    K2 = 2 * nk
    J = NH * iheads
    base = wide - 128
    tail = width - base
    scale = width ** -0.5
    inv_scale = width ** 0.5
    log2e = math.log2(math.e)
    own_plane = x == zl

    def ctx_of(zl_, y_, c_):
        return (zl_ * NY + y_) * 2 + c_

    def rcopy(src, dst, ssem, rsem, ctx_, head_):
        return pltpu.make_async_remote_copy(
            src_ref=src, dst_ref=dst, send_sem=ssem, recv_sem=rsem,
            device_id={"ctx": ctx_, "head": head_}, device_id_type=MESH,
        )

    def arrived(dst, rsem):
        pltpu.make_async_copy(dst, dst, rsem).wait()

    sends = []

    def send(*args):
        cp = rcopy(*args)
        cp.start()
        sends.append(cp.wait_send)

    def send_unless(local, src, dst, ssem, rsem, ctx_, head_):
        @pl.when(jnp.logical_not(local))
        def _():
            rcopy(src, dst, ssem, rsem, ctx_, head_).start()

        @pl.when(local)
        def _():
            pltpu.make_async_copy(src, dst, rsem).start()

        def finish():
            @pl.when(jnp.logical_not(local))
            def _():
                rcopy(src, dst, ssem, rsem, ctx_, head_).wait_send()

        sends.append(finish)

    y_peers = [lax.rem(y + d, NY) for d in range(1, NY)]
    z_peers = [lax.rem(zl + d, NZ) for d in range(1, NZ)]
    x_peers = [lax.rem(x + d, NX) for d in range(1, NX)]
    zls = [zl] + z_peers
    hs = [lax.rem(head + d, NH) for d in range(NH)]

    barrier = pltpu.get_barrier_semaphore()

    def greet(ctx_, head_):
        pl.semaphore_signal(barrier, inc=1, device_id={"ctx": ctx_, "head": head_}, device_id_type=MESH)

    for d, h in enumerate(hs):
        if d == 0:
            @pl.when(jnp.logical_not(own_plane))
            def _():
                greet(ctx_of(x, y, c), head)
        else:
            greet(ctx_of(x, y, c), h)
    for r in range(NZH):
        for d, z_ in enumerate(zls):
            if d == 0:
                @pl.when(jnp.logical_not(own_plane & (zh == r)))
                def _():
                    greet(ctx_of(zl, y, c), r * NX + zl)
            else:
                greet(ctx_of(z_, y, c), r * NX + zl)
    greet(ctx_of(zl, y, 1 - c), head)
    for y_ in y_peers:
        greet(ctx_of(zl, y_, c), head)
    for z_ in z_peers:
        greet(ctx_of(z_, y, c), head)
    for x_ in x_peers:
        greet(ctx, zh * NX + x_)
    greet(ctx, (1 - zh) * NX + x)
    n_greet = 1 + (NY - 1) + (NZ - 1) + (NX - 1) + 1 + NH + NZH * NZ

    lane = lax.broadcasted_iota(jnp.int32, (heads, 128), 1)
    for r in range(rows):
        t3 = list(split3(column(lse_ref[r : r + 1, :])))
        w3 = [jnp.concatenate([v, jnp.zeros((heads - iheads, 1), F32)], axis=0)
              for v in split3(column(w_ref[r : r + 1, :]))]
        aug = jnp.zeros((heads, 128), F32)
        for n, v in enumerate(t3 + w3):
            aug = jnp.where(lane == tail + n, v, aug)
        q_stage[r, :, :base] = q_ref[r, :, :base]
        last = jnp.concatenate([q_ref[r, :, base:].astype(F32), jnp.zeros((heads, 128 - tail), F32)], axis=1)
        q_stage[r, :, base:] = (last + aug).astype(BF16)
        i_stage[r] = jnp.concatenate(
            [qi_ref[r].astype(F32), jnp.zeros((heads - iheads, idim), F32)], axis=0
        ).astype(BF16)
    krow = lax.broadcasted_iota(jnp.int32, (wide - width, nk), 0)
    latbuf[0, :width] = lat_ref[...]
    for side in range(2):
        latbuf[side, width:] = jnp.where(krow < 3, -inv_scale, 0.0).astype(BF16)
    kbuf[0] = k_ref[...]

    pl.semaphore_wait(barrier, jnp.where(own_plane, n_greet - 2, n_greet))

    for r in range(rows):
        for d, z_ in enumerate(zls):
            to = (ctx_of(z_, y, c), r * NX + zl)
            iargs = (i_stage.at[r], ientry.at[head], s_ei.at[r, d], r_ei.at[head], *to)
            qargs = (q_stage.at[r], qbuf.at[y, head], s_eq.at[r, d], r_eq.at[head], *to)
            if d == 0:
                send_unless(own_plane & (zh == r), *iargs)
                send_unless(own_plane & (zh == r), *qargs)
            else:
                send(*iargs)
                send(*qargs)
    other = ctx_of(zl, y, 1 - c)
    send(kbuf.at[0], kbuf.at[1], s_core.at[0], r_core.at[0], other, head)
    send(latbuf.at[0, :width], latbuf.at[1, :width], s_core.at[1], r_core.at[1], other, head)

    NC = NH // 2
    up, down = lax.rem(y + 1, NY), lax.rem(y + NY - 1, NY)
    half_up = NY // 2
    half_down = NY - 1 - half_up

    def piece(y0, n):
        return ibuf.at[y0] if n == 0 else qbuf.at[y0, 2 * (n - 1) : 2 * n]

    def forward(y0, n, step, plus, minus):
        if plus:
            send(piece(y0, n), piece(y0, n), s_up.at[step, n], r_y.at[y0, n], ctx_of(zl, up, c), head)
        if minus:
            send(piece(y0, n), piece(y0, n), s_down.at[step, n], r_y.at[y0, n], ctx_of(zl, down, c), head)

    for h in range(NH):
        arrived(ientry.at[h], r_ei.at[h])
    ibuf[y] = ientry[...].astype(F32)[:, :iheads, :].reshape(J, idim).astype(BF16)
    forward(y, 0, 0, half_up > 0, half_down > 0)
    for n in range(NC):
        for h in (2 * n, 2 * n + 1):
            arrived(qbuf.at[y, h], r_eq.at[h])
        forward(y, n + 1, 0, half_up > 0, half_down > 0)

    CH = min(512, nk)

    def block(y0):
        q = qbuf[y0].reshape(NH * heads, wide)
        qi = ibuf[y0]
        aug = qbuf[y0, :, :, base:].astype(F32).reshape(NH * heads, 128)
        ln = lax.broadcasted_iota(jnp.int32, aug.shape, 1)
        wide_col = jnp.sum(jnp.where((ln >= tail + 3) & (ln < tail + 6), aug, 0.0), axis=1, keepdims=True)
        wcol = wide_col.reshape(NH, heads, 1)[:, :iheads, :].reshape(J, 1)
        wq[y0] = (qi.astype(F32) * wcol).astype(BF16)
        for side in range(2):
            for n in range(nk // CH):
                cols = slice(n * CH, (n + 1) * CH)
                kcols = slice(side * nk + n * CH, side * nk + (n + 1) * CH)
                s = jnp.dot(q, latbuf[side, :, cols], preferred_element_type=F32)
                e = jnp.exp2(s * (scale * log2e))
                tacc[y0, :, kcols] = jnp.sum(e.reshape(NH * heads // 8, 8, CH), axis=0)
                rw = lax.dot_general(qi, kbuf[side, cols, :], NT, preferred_element_type=F32)
                raw[y0, :, kcols] = rw
                sacc[y0, :, kcols] = jnp.sum((wcol * jnp.maximum(rw, 0.0)).reshape(J // 8, 8, CH), axis=0)

    arrived(kbuf.at[1], r_core.at[0])
    arrived(latbuf.at[1, :width], r_core.at[1])
    block(y)
    for step in range(1, half_up + 1):
        yu = lax.rem(y + NY - step, NY)
        yd = lax.rem(y + step, NY)
        for n in range(NC + 1):
            arrived(piece(yu, n), r_y.at[yu, n])
            forward(yu, n, step, step < half_up, False)
            if step <= half_down:
                arrived(piece(yd, n), r_y.at[yd, n])
                forward(yd, n, step, False, step < half_down)
        block(yu)
        if step <= half_down:
            block(yd)

    target = jnp.sum(tacc[...], axis=1)
    score = jnp.sum(sacc[...], axis=1)
    m = jnp.max(score, axis=1, keepdims=True)
    l = jnp.sum(jnp.exp(score - m), axis=1, keepdims=True)
    t = jnp.sum(target, axis=1, keepdims=True)
    sl = lax.broadcasted_iota(jnp.int32, (NY, 128), 1)

    def exchange(buf, me, peers, where, ssem, rsem, m, l, t):
        buf[me] = jnp.where(sl == 0, m, jnp.where(sl == 1, l, t))
        for n, p in enumerate(peers):
            send(buf.at[me], buf.at[me], ssem.at[n], rsem.at[me], where(p), head)
        for p in peers:
            arrived(buf.at[p], rsem.at[p])
        all_ = buf[...]
        mm = jnp.max(all_[:, :, 0:1], axis=0)
        ll = jnp.sum(all_[:, :, 1:2] * jnp.exp(all_[:, :, 0:1] - mm[None]), axis=0)
        tt = jnp.sum(all_[:, :, 2:3], axis=0)
        return mm, ll, tt

    m, l, t = exchange(sy_buf, y, y_peers, lambda p: ctx_of(zl, p, c), s_sy, r_sy, m, l, t)
    m, l, t = exchange(sz_buf, zl, z_peers, lambda p: ctx_of(p, y, c), s_sz, r_sz, m, l, t)
    grad = factor * (jnp.exp(score - m) / l - target / t)
    gbuf[...] = grad.astype(BF16).astype(F32)

    wqt = wq[...].reshape(NY * J, idim).astype(F32).T.astype(BF16)

    def mask_half(side):
        kcols = slice(side * nk, (side + 1) * nk)
        for y0 in range(NY):
            g = jnp.where(raw[y0, :, kcols] > 0, gbuf[y0 : y0 + 1, kcols], 0.0)
            masked[side, y0 * J : (y0 + 1) * J] = g.astype(BF16)

    mask_half(1)
    ck_send[...] = jnp.dot(wqt, masked[1], preferred_element_type=F32).astype(BF16)
    send(ck_send, ck_recv, s_core.at[2], r_core.at[2], other, head)
    mask_half(0)
    nq = nk // NX
    own_key = jnp.dot(wqt, masked[0], preferred_element_type=F32)
    arrived(ck_recv, r_core.at[2])
    for n in range(NX):
        v = own_key[:, n * nq : (n + 1) * nq] + ck_recv[:, n * nq : (n + 1) * nq].astype(F32)
        gx_sum[n] = v
        gx_send[n] = v.astype(BF16)
    for n, x_ in enumerate(x_peers):
        send(gx_send.at[x_], gx_recv.at[x], s_gx.at[n], r_gx.at[x], ctx, zh * NX + x_)

    part[...] = (
        jnp.dot(masked[0], kbuf[0], preferred_element_type=F32)
        + jnp.dot(masked[1], kbuf[1], preferred_element_type=F32)
    ).reshape(part.shape).astype(part.dtype)
    for n, y_ in enumerate(y_peers):
        send(part.at[y_], ry_buf.at[y], s_ry.at[n], r_ry.at[y], ctx_of(zl, y_, c), head)

    gsum = gx_sum[x]
    for x_ in x_peers:
        arrived(gx_recv.at[x_], r_gx.at[x_])
        gsum = gsum + gx_recv[x_].astype(F32)
    gz_send[...] = gsum.astype(BF16)
    send(gz_send, gz_recv, s_gz.at[0], r_gz.at[0], ctx, (1 - zh) * NX + x)

    total = part[y].astype(F32)
    for y_ in y_peers:
        arrived(ry_buf.at[y_], r_ry.at[y_])
        total = total + ry_buf[y_].astype(F32)
    zsum[...] = total.reshape(zsum.shape)
    slot = zh * NZ + zl
    for d, h in enumerate(hs):
        args = (zsum.at[h], fq_buf.at[slot], s_fq.at[d], r_fq.at[slot], ctx_of(x, y, c), h)
        if d == 0:
            send_unless(own_plane, *args)
        else:
            send(*args)

    arrived(gz_recv, r_gz.at[0])
    ga_buf[x] = (gz_send[...].astype(F32) + gz_recv[...].astype(F32)).T.astype(BF16)
    for n, x_ in enumerate(x_peers):
        send(ga_buf.at[x], ga_buf.at[x], s_ga.at[n], r_ga.at[x], ctx, zh * NX + x_)

    for n in range(NZH * NZ):
        arrived(fq_buf.at[n], r_fq.at[n])
    for r in range(rows):
        own = jnp.sum(fq_buf[r * NZ : (r + 1) * NZ], axis=0)
        gq_ref[r] = own * column(w_ref[r : r + 1, :])
        gw_ref[r : r + 1, :] = row_of(jnp.sum(own * qi_ref[r].astype(F32), axis=1, keepdims=True))

    for x_ in x_peers:
        arrived(ga_buf.at[x_], r_ga.at[x_])
    gk_ref[...] = ga_buf[...].astype(F32).reshape(gk_ref.shape)

    for finish in sends:
        finish()


def body(dims, keys, q_attn, latent, lse_saved, q_index, k_index, head_weight):
    NZ, NY, NZH, NX = dims
    NH = NZH * NX
    rows, heads, width = q_attn.shape
    iheads, idim = q_index.shape[1:]
    nk = latent.shape[0]
    wide = -(-width // 128) * 128
    J = NH * iheads
    K2 = 2 * nk
    nq = nk // NX
    NP = NH // 2 + 1
    V, DMA = pltpu.VMEM, pltpu.SemaphoreType.DMA
    vm = pl.BlockSpec(memory_space=pltpu.VMEM)
    scratch = [
        V((rows, heads, wide), BF16), V((rows, heads, idim), BF16),
        V((NY, NH, heads, wide), BF16), V((NH, heads, idim), BF16), V((NY, J, idim), BF16),
        V((2, wide, nk), BF16), V((2, nk, idim), BF16),
        V((NY, J, K2), F32), V((NY, J, idim), BF16),
        V((NY, 8, K2), F32), V((NY, 8, K2), F32), V((NY, K2), F32), V((2, NY * J, nk), BF16),
        V((NY, NY, 128), F32), V((NZ, NY, 128), F32),
        V((NY, J, idim), BF16), V((NY, J, idim), BF16),
        V((NH, iheads, idim), F32), V((NZH * NZ, iheads, idim), F32),
        V((idim, nk), BF16), V((idim, nk), BF16),
        V((NX, idim, nq), F32), V((NX, idim, nq), BF16), V((NX, idim, nq), BF16),
        V((idim, nq), BF16), V((idim, nq), BF16), V((NX, nq, idim), BF16),
        DMA((rows, NZ)), DMA((rows, NZ)), DMA((NH,)), DMA((NH,)), DMA((3,)), DMA((3,)),
        DMA((NY, NP)), DMA((NY, NP)), DMA((NY, NP)),
        DMA((NY,)), DMA((NY,)), DMA((NZ,)), DMA((NZ,)), DMA((NY,)), DMA((NY,)), DMA((NH,)), DMA((NZH * NZ,)),
        DMA((NX,)), DMA((NX,)), DMA((1,)), DMA((1,)), DMA((NX,)), DMA((NX,)),
    ]
    return pl.pallas_call(
        functools.partial(kernel, dims, keys / 32.0),
        out_shape=(
            jax.ShapeDtypeStruct((rows, iheads, idim), F32),
            jax.ShapeDtypeStruct((rows, iheads), F32),
            jax.ShapeDtypeStruct((nk, idim), F32),
        ),
        in_specs=[vm] * 6,
        out_specs=(vm, vm, vm),
        scratch_shapes=scratch,
        compiler_params=pltpu.CompilerParams(
            collective_id=0, has_side_effects=True, vmem_limit_bytes=48 * 1024 * 1024
        ),
        name="indexer_backward",
    )(q_attn, latent.T, lse_saved, q_index, k_index, head_weight)


def build(mesh, dims, keys):
    return jax.shard_map(
        functools.partial(body, dims, keys),
        mesh=mesh,
        in_specs=(
            P("ctx", "head", None),
            P("ctx", None),
            P("ctx", "head"),
            P("ctx", "head", None),
            P("ctx", None),
            P("ctx", "head"),
        ),
        out_specs=(P("ctx", "head", None), P("ctx", "head"), P("ctx", None)),
        check_vma=False,
    )


def solution(mesh):
    return build(mesh, DIMS, 65536)
```

time: 85.6 us -> 79.9 us (0.933)
  Pallas kernels: 80.2 us -> 71.8 us
  local copies, waits for them, and re-layouts: 3.7 us -> 6.99 us
    pallas_call x1, Pallas kernels: 80.2 us -> 71.8 us  [body(): pl.pallas_call(functools.partial(kernel, dims, keys / 32.0), out_shape=(j...]
    unnamed x14 -> x15, local copies, waits for them, and re-layouts: 3.7 us -> 6.99 us
where the time goes in v2:
time: 79.9 us; the launch traced here: 79.5 us
  Pallas kernels  71.8 us (90%)
  local copies, waits for them, and re-layouts  6.99 us (9%)
    pallas_call x1, Pallas kernels, body(): pl.pallas_call(functools.partial(kernel, dims, keys / 32.0), out_shape=(j...  71.8 us
    unnamed x15, local copies, waits for them, and re-layouts  6.99 us

profile of v2, /device:TPU:1, one launch (start us, length us, event | category | flops | bytes accessed | tf_op | source)
XLA Modules:
  0.0 79.5 jit_solution(5278626498693835630)
XLA Ops:
  0.6 0.0 copy-start
  0.6 1.3 %copy-done = bf16[1024,576]{0,1:T(8,128)(2,1)S(1)} copy-done((bf16[1024,576]{0,1:T(8,128)(2,1)S(1)}, bf16[1024,576]{0,1:T(8,128)(2,1)}, u32[]{:S(2)}) %copy-start) | copy-done | bytes 1179672
  1.9 0.0 copy-start.1
  1.9 0.9 %copy-done.1 = bf16[1024,128]{1,0:T(8,128)(2,1)S(1)} copy-done((bf16[1024,128]{1,0:T(8,128)(2,1)S(1)}, bf16[1024,128]{1,0:T(8,128)(2,1)}, u32[]{:S(2)}) %copy-start.1) | copy-done | bytes 262168
  2.9 0.0 copy-start.2
  2.9 0.8 copy-done.2
  3.6 0.0 copy-start.3
  3.6 0.7 copy-done.3
  4.3 0.0 copy-start.4
  4.3 0.7 copy-done.4
  5.0 0.0 copy-start.5
  5.0 0.7 copy-done.5
  5.7 71.8 %indexer_backward.1 = (f32[2,8,128]{2,1,0:T(8,128)S(1)}, f32[2,8]{1,0:T(2,128)S(1)}, f32[1024,128]{1,0:T(8,128)S(1)}) custom-call(bf16[2,16,576]{2,1,0:T(8,128)(2,1)S(1)} %copy-done.2, bf16[576,1024]{1,0:T(8,128)(2,1)S(1)} %bitcast.1, f32[2,16]{1,0:T(2,128)S(1)} %copy-done.4, bf16[2,8,128]{2,1,0:T(8,128)(2,1)S(1)} %copy-done.3, ...), custom_call_target="tpu_custom_call" | custom-call | tf_op jit(solution)/shard_map/indexer_backward/pallas_call | solution.py:357
  77.5 0.6 copy.12
  78.1 0.6 copy.13
  78.7 0.8 copy.14
Async XLA Ops:
  0.6 1.3 %copy-start = (bf16[1024,576]{0,1:T(8,128)(2,1)S(1)}, bf16[1024,576]{0,1:T(8,128)(2,1)}, u32[]{:S(2)}) copy-start(bf16[1024,576]{0,1:T(8,128)(2,1)} %param.7) | copy-start | bytes 3538948
  1.9 0.9 %copy-start.1 = (bf16[1024,128]{1,0:T(8,128)(2,1)S(1)}, bf16[1024,128]{1,0:T(8,128)(2,1)}, u32[]{:S(2)}) copy-start(bf16[1024,128]{1,0:T(8,128)(2,1)} %k_ref.1) | copy-start | bytes 786436
  2.9 0.8 copy-start.2
  3.6 0.7 copy-start.3
  4.3 0.7 copy-start.4
  5.0 0.7 copy-start.5

commit v3 on v2

--- a/solution.py
+++ b/solution.py
@@ -11,6 +11,7 @@
 MESH = pl.DeviceIdType.MESH
 F32, BF16 = jnp.float32, jnp.bfloat16
 DIMS = (4, 8, 2, 4)
+KC = 2
 NT = (((1,), (1,)), ((), ()))
 
 
@@ -34,13 +35,14 @@
 
 def kernel(
     dims, factor,
-    q_ref, lat_ref, lse_ref, qi_ref, k_ref, w_ref,
+    q_hbm, lat_hbm, lse_hbm, qi_hbm, k_hbm, w_hbm,
     gq_ref, gw_ref, gk_ref,
+    q_ref, lse_ref, qi_ref, w_ref, s_in,
     q_stage, i_stage, qbuf, ientry, ibuf, latbuf, kbuf, raw, wq, tacc, sacc, gbuf, masked,
-    sy_buf, sz_buf, part, ry_buf, zsum, fq_buf,
+    st_buf, part, ry_buf, zsum, fq_buf,
     ck_send, ck_recv, gx_sum, gx_send, gx_recv, gz_send, gz_recv, ga_buf,
-    s_eq, s_ei, r_eq, r_ei, s_core, r_core, s_up, s_down, r_y,
-    s_sy, r_sy, s_sz, r_sz, s_ry, r_ry, s_fq, r_fq, s_gx, r_gx, s_gz, r_gz, s_ga, r_ga,
+    s_eq, s_ei, r_eq, r_ei, s_core, r_core, s_ck, r_ck, s_up, s_down, r_y,
+    s_st, r_st, s_ry, r_ry, s_fq, r_fq, s_gx, r_gx, s_gz, r_gz, s_ga, r_ga,
 ):
     NZ, NY, NZH, NX = dims
     NH = NZH * NX
@@ -52,7 +54,7 @@
     zh = lax.div(head, NX)
     rows, heads, width = q_ref.shape
     iheads, idim = qi_ref.shape[1:]
-    nk = lat_ref.shape[1]
+    nk = lat_hbm.shape[1]
     wide = qbuf.shape[-1]
     K2 = 2 * nk
     J = NH * iheads
@@ -102,7 +104,21 @@
     z_peers = [lax.rem(zl + d, NZ) for d in range(1, NZ)]
     x_peers = [lax.rem(x + d, NX) for d in range(1, NX)]
     zls = [zl] + z_peers
+    plane = [
+        (ctx_of(lax.rem(zl + dz, NZ), lax.rem(y + dy, NY), c), lax.rem(zl + dz, NZ) * NY + lax.rem(y + dy, NY))
+        for dy in sorted(range(NY), key=lambda d: -min(d, NY - d)) for dz in range(NZ) if dy or dz
+    ]
     hs = [lax.rem(head + d, NH) for d in range(NH)]
+
+    loads = [
+        pltpu.make_async_copy(src, dst, s_in.at[n])
+        for n, (src, dst) in enumerate((
+            (q_hbm, q_ref), (lse_hbm, lse_ref), (qi_hbm, qi_ref), (w_hbm, w_ref),
+            (k_hbm, kbuf.at[0]), (lat_hbm, latbuf.at[0, :width]),
+        ))
+    ]
+    for cp in loads:
+        cp.start()
 
     barrier = pltpu.get_barrier_semaphore()
 
@@ -125,15 +141,15 @@
             else:
                 greet(ctx_of(z_, y, c), r * NX + zl)
     greet(ctx_of(zl, y, 1 - c), head)
-    for y_ in y_peers:
-        greet(ctx_of(zl, y_, c), head)
-    for z_ in z_peers:
-        greet(ctx_of(z_, y, c), head)
+    for p in plane:
+        greet(p[0], head)
     for x_ in x_peers:
         greet(ctx, zh * NX + x_)
     greet(ctx, (1 - zh) * NX + x)
-    n_greet = 1 + (NY - 1) + (NZ - 1) + (NX - 1) + 1 + NH + NZH * NZ
-
+    n_greet = 1 + (NY * NZ - 1) + (NX - 1) + 1 + NH + NZH * NZ
+
+    for cp in loads[:4]:
+        cp.wait()
     lane = lax.broadcasted_iota(jnp.int32, (heads, 128), 1)
     for r in range(rows):
         t3 = list(split3(column(lse_ref[r : r + 1, :])))
@@ -149,14 +165,14 @@
             [qi_ref[r].astype(F32), jnp.zeros((heads - iheads, idim), F32)], axis=0
         ).astype(BF16)
     krow = lax.broadcasted_iota(jnp.int32, (wide - width, nk), 0)
-    latbuf[0, :width] = lat_ref[...]
     for side in range(2):
         latbuf[side, width:] = jnp.where(krow < 3, -inv_scale, 0.0).astype(BF16)
-    kbuf[0] = k_ref[...]
+    for cp in loads[4:]:
+        cp.wait()
 
     pl.semaphore_wait(barrier, jnp.where(own_plane, n_greet - 2, n_greet))
 
-    for r in range(rows):
+    for r in (1 - zh, zh) if NZH == 2 else range(NZH):
         for d, z_ in enumerate(zls):
             to = (ctx_of(z_, y, c), r * NX + zl)
             iargs = (i_stage.at[r], ientry.at[head], s_ei.at[r, d], r_ei.at[head], *to)
@@ -173,26 +189,33 @@
 
     NC = NH // 2
     up, down = lax.rem(y + 1, NY), lax.rem(y + NY - 1, NY)
-    half_up = NY // 2
-    half_down = NY - 1 - half_up
+    far = NY // 2
+    near = far - 1
+    order = [lax.rem(zh * (NC // 2) + n, NC) for n in range(NC)]
+    order.insert(NC // 2, NC)
 
     def piece(y0, n):
-        return ibuf.at[y0] if n == 0 else qbuf.at[y0, 2 * (n - 1) : 2 * n]
-
-    def forward(y0, n, step, plus, minus):
+        return ibuf.at[y0] if n is NC else qbuf.at[y0, pl.ds(2 * n, 2)]
+
+    def forward(y0, k, step, plus, minus):
+        n = order[k]
         if plus:
-            send(piece(y0, n), piece(y0, n), s_up.at[step, n], r_y.at[y0, n], ctx_of(zl, up, c), head)
+            send(piece(y0, n), piece(y0, n), s_up.at[step, k], r_y.at[y0, n], ctx_of(zl, up, c), head)
         if minus:
-            send(piece(y0, n), piece(y0, n), s_down.at[step, n], r_y.at[y0, n], ctx_of(zl, down, c), head)
-
-    for h in range(NH):
-        arrived(ientry.at[h], r_ei.at[h])
-    ibuf[y] = ientry[...].astype(F32)[:, :iheads, :].reshape(J, idim).astype(BF16)
-    forward(y, 0, 0, half_up > 0, half_down > 0)
-    for n in range(NC):
-        for h in (2 * n, 2 * n + 1):
-            arrived(qbuf.at[y, h], r_eq.at[h])
-        forward(y, n + 1, 0, half_up > 0, half_down > 0)
+            send(piece(y0, n), piece(y0, n), s_down.at[step, k], r_y.at[y0, n], ctx_of(zl, down, c), head)
+
+    def by_up(k):
+        return k <= NC // 2
+
+    for k, n in enumerate(order):
+        if n is NC:
+            for h in range(NH):
+                arrived(ientry.at[h], r_ei.at[h])
+            ibuf[y] = ientry[...].astype(F32)[:, :iheads, :].reshape(J, idim).astype(BF16)
+        else:
+            for h in (2 * n, 2 * n + 1):
+                arrived(qbuf.at[y, h], r_eq.at[h])
+        forward(y, k, 0, near > 0 or by_up(k), near > 0 or not by_up(k))
 
     CH = min(512, nk)
 
@@ -218,18 +241,20 @@
     arrived(kbuf.at[1], r_core.at[0])
     arrived(latbuf.at[1, :width], r_core.at[1])
     block(y)
-    for step in range(1, half_up + 1):
+    for step in range(1, near + 1):
         yu = lax.rem(y + NY - step, NY)
         yd = lax.rem(y + step, NY)
-        for n in range(NC + 1):
+        for k, n in enumerate(order):
             arrived(piece(yu, n), r_y.at[yu, n])
-            forward(yu, n, step, step < half_up, False)
-            if step <= half_down:
-                arrived(piece(yd, n), r_y.at[yd, n])
-                forward(yd, n, step, False, step < half_down)
+            forward(yu, k, step, step < near or by_up(k), False)
+            arrived(piece(yd, n), r_y.at[yd, n])
+            forward(yd, k, step, False, step < near or not by_up(k))
         block(yu)
-        if step <= half_down:
-            block(yd)
+        block(yd)
+    yf = lax.rem(y + far, NY)
+    for n in order:
+        arrived(piece(yf, n), r_y.at[yf, n])
+    block(yf)
 
     target = jnp.sum(tacc[...], axis=1)
     score = jnp.sum(sacc[...], axis=1)
@@ -237,45 +262,50 @@
     l = jnp.sum(jnp.exp(score - m), axis=1, keepdims=True)
     t = jnp.sum(target, axis=1, keepdims=True)
     sl = lax.broadcasted_iota(jnp.int32, (NY, 128), 1)
-
-    def exchange(buf, me, peers, where, ssem, rsem, m, l, t):
-        buf[me] = jnp.where(sl == 0, m, jnp.where(sl == 1, l, t))
-        for n, p in enumerate(peers):
-            send(buf.at[me], buf.at[me], ssem.at[n], rsem.at[me], where(p), head)
-        for p in peers:
-            arrived(buf.at[p], rsem.at[p])
-        all_ = buf[...]
-        mm = jnp.max(all_[:, :, 0:1], axis=0)
-        ll = jnp.sum(all_[:, :, 1:2] * jnp.exp(all_[:, :, 0:1] - mm[None]), axis=0)
-        tt = jnp.sum(all_[:, :, 2:3], axis=0)
-        return mm, ll, tt
-
-    m, l, t = exchange(sy_buf, y, y_peers, lambda p: ctx_of(zl, p, c), s_sy, r_sy, m, l, t)
-    m, l, t = exchange(sz_buf, zl, z_peers, lambda p: ctx_of(p, y, c), s_sz, r_sz, m, l, t)
+    ss = lax.broadcasted_iota(jnp.int32, (NY, 128), 0)
+    at = [sl == ss + n * NY for n in range(3)]
+    me = zl * NY + y
+    mine = jnp.where(at[0], m, jnp.where(at[1], l, jnp.where(at[2], t, 0.0)))
+    st_buf[pl.ds(me, 1), :] = jnp.sum(mine, axis=0, keepdims=True)
+    for n, (dev, _) in enumerate(plane):
+        send(st_buf.at[pl.ds(me, 1)], st_buf.at[pl.ds(me, 1)], s_st.at[n], r_st.at[me], dev, head)
+    wqt = wq[...].reshape(NY * J, idim).astype(F32).T.astype(BF16)
+    for _, slot in plane:
+        arrived(st_buf.at[pl.ds(slot, 1)], r_st.at[slot])
+    stats = st_buf[...]
+    peak = pltpu.roll(stats, NY, 1)
+    top = jnp.max(peak, axis=0, keepdims=True)
+    in_l = lax.broadcasted_iota(jnp.int32, stats.shape, 1) // NY == 1
+    mass = jnp.sum(jnp.where(in_l, stats * jnp.exp(jnp.where(in_l, peak - top, 0.0)), stats), axis=0, keepdims=True)
+    m = jnp.sum(jnp.where(at[1], top, 0.0), axis=1, keepdims=True)
+    l = jnp.sum(jnp.where(at[1], mass, 0.0), axis=1, keepdims=True)
+    t = jnp.sum(jnp.where(at[2], mass, 0.0), axis=1, keepdims=True)
     grad = factor * (jnp.exp(score - m) / l - target / t)
     gbuf[...] = grad.astype(BF16).astype(F32)
 
-    wqt = wq[...].reshape(NY * J, idim).astype(F32).T.astype(BF16)
-
-    def mask_half(side):
-        kcols = slice(side * nk, (side + 1) * nk)
+    nc = nk // KC
+    nq = nc // NX
+
+    def mask(side, q):
+        cols = slice(q * nc, (q + 1) * nc)
+        kcols = slice(side * nk + q * nc, side * nk + (q + 1) * nc)
         for y0 in range(NY):
             g = jnp.where(raw[y0, :, kcols] > 0, gbuf[y0 : y0 + 1, kcols], 0.0)
-            masked[side, y0 * J : (y0 + 1) * J] = g.astype(BF16)
-
-    mask_half(1)
-    ck_send[...] = jnp.dot(wqt, masked[1], preferred_element_type=F32).astype(BF16)
-    send(ck_send, ck_recv, s_core.at[2], r_core.at[2], other, head)
-    mask_half(0)
-    nq = nk // NX
-    own_key = jnp.dot(wqt, masked[0], preferred_element_type=F32)
-    arrived(ck_recv, r_core.at[2])
-    for n in range(NX):
-        v = own_key[:, n * nq : (n + 1) * nq] + ck_recv[:, n * nq : (n + 1) * nq].astype(F32)
-        gx_sum[n] = v
-        gx_send[n] = v.astype(BF16)
-    for n, x_ in enumerate(x_peers):
-        send(gx_send.at[x_], gx_recv.at[x], s_gx.at[n], r_gx.at[x], ctx, zh * NX + x_)
+            masked[side, y0 * J : (y0 + 1) * J, cols] = g.astype(BF16)
+        return jnp.dot(wqt, masked[side, :, cols], preferred_element_type=F32)
+
+    for q in range(KC):
+        ck_send[q] = mask(1, q).astype(BF16)
+        send(ck_send.at[q], ck_recv.at[q], s_ck.at[q], r_ck.at[q], other, head)
+    for q in range(KC):
+        own_key = mask(0, q)
+        arrived(ck_recv.at[q], r_ck.at[q])
+        own_key = own_key + ck_recv[q].astype(F32)
+        for n in range(NX):
+            gx_sum[q, n] = own_key[:, n * nq : (n + 1) * nq]
+            gx_send[q, n] = own_key[:, n * nq : (n + 1) * nq].astype(BF16)
+        for n, x_ in enumerate(x_peers):
+            send(gx_send.at[q, x_], gx_recv.at[q, x], s_gx.at[q, n], r_gx.at[q, x], ctx, zh * NX + x_)
 
     part[...] = (
         jnp.dot(masked[0], kbuf[0], preferred_element_type=F32)
@@ -284,12 +314,13 @@
     for n, y_ in enumerate(y_peers):
         send(part.at[y_], ry_buf.at[y], s_ry.at[n], r_ry.at[y], ctx_of(zl, y_, c), head)
 
-    gsum = gx_sum[x]
-    for x_ in x_peers:
-        arrived(gx_recv.at[x_], r_gx.at[x_])
-        gsum = gsum + gx_recv[x_].astype(F32)
-    gz_send[...] = gsum.astype(BF16)
-    send(gz_send, gz_recv, s_gz.at[0], r_gz.at[0], ctx, (1 - zh) * NX + x)
+    for q in range(KC):
+        gsum = gx_sum[q, x]
+        for x_ in x_peers:
+            arrived(gx_recv.at[q, x_], r_gx.at[q, x_])
+            gsum = gsum + gx_recv[q, x_].astype(F32)
+        gz_send[q] = gsum.astype(BF16)
+        send(gz_send.at[q], gz_recv.at[q], s_gz.at[q], r_gz.at[q], ctx, (1 - zh) * NX + x)
 
     total = part[y].astype(F32)
     for y_ in y_peers:
@@ -304,10 +335,11 @@
         else:
             send(*args)
 
-    arrived(gz_recv, r_gz.at[0])
-    ga_buf[x] = (gz_send[...].astype(F32) + gz_recv[...].astype(F32)).T.astype(BF16)
-    for n, x_ in enumerate(x_peers):
-        send(ga_buf.at[x], ga_buf.at[x], s_ga.at[n], r_ga.at[x], ctx, zh * NX + x_)
+    for q in range(KC):
+        arrived(gz_recv.at[q], r_gz.at[q])
+        ga_buf[q, x] = (gz_send[q].astype(F32) + gz_recv[q].astype(F32)).T.astype(BF16)
+        for n, x_ in enumerate(x_peers):
+            send(ga_buf.at[q, x], ga_buf.at[q, x], s_ga.at[q, n], r_ga.at[q, x], ctx, zh * NX + x_)
 
     for n in range(NZH * NZ):
         arrived(fq_buf.at[n], r_fq.at[n])
@@ -316,8 +348,9 @@
         gq_ref[r] = own * column(w_ref[r : r + 1, :])
         gw_ref[r : r + 1, :] = row_of(jnp.sum(own * qi_ref[r].astype(F32), axis=1, keepdims=True))
 
-    for x_ in x_peers:
-        arrived(ga_buf.at[x_], r_ga.at[x_])
+    for q in range(KC):
+        for x_ in x_peers:
+            arrived(ga_buf.at[q, x_], r_ga.at[q, x_])
     gk_ref[...] = ga_buf[...].astype(F32).reshape(gk_ref.shape)
 
     for finish in sends:
@@ -333,26 +366,27 @@
     wide = -(-width // 128) * 128
     J = NH * iheads
     K2 = 2 * nk
-    nq = nk // NX
+    nq = nk // NX // KC
     NP = NH // 2 + 1
     V, DMA = pltpu.VMEM, pltpu.SemaphoreType.DMA
     vm = pl.BlockSpec(memory_space=pltpu.VMEM)
     scratch = [
+        V((rows, heads, width), BF16), V((rows, heads), F32), V((rows, iheads, idim), BF16), V((rows, iheads), F32), DMA((6,)),
         V((rows, heads, wide), BF16), V((rows, heads, idim), BF16),
         V((NY, NH, heads, wide), BF16), V((NH, heads, idim), BF16), V((NY, J, idim), BF16),
         V((2, wide, nk), BF16), V((2, nk, idim), BF16),
         V((NY, J, K2), F32), V((NY, J, idim), BF16),
         V((NY, 8, K2), F32), V((NY, 8, K2), F32), V((NY, K2), F32), V((2, NY * J, nk), BF16),
-        V((NY, NY, 128), F32), V((NZ, NY, 128), F32),
+        V((NZ * NY, 128), F32),
         V((NY, J, idim), BF16), V((NY, J, idim), BF16),
         V((NH, iheads, idim), F32), V((NZH * NZ, iheads, idim), F32),
-        V((idim, nk), BF16), V((idim, nk), BF16),
-        V((NX, idim, nq), F32), V((NX, idim, nq), BF16), V((NX, idim, nq), BF16),
-        V((idim, nq), BF16), V((idim, nq), BF16), V((NX, nq, idim), BF16),
-        DMA((rows, NZ)), DMA((rows, NZ)), DMA((NH,)), DMA((NH,)), DMA((3,)), DMA((3,)),
+        V((KC, idim, nk // KC), BF16), V((KC, idim, nk // KC), BF16),
+        V((KC, NX, idim, nq), F32), V((KC, NX, idim, nq), BF16), V((KC, NX, idim, nq), BF16),
+        V((KC, idim, nq), BF16), V((KC, idim, nq), BF16), V((KC, NX, nq, idim), BF16),
+        DMA((rows, NZ)), DMA((rows, NZ)), DMA((NH,)), DMA((NH,)), DMA((2,)), DMA((2,)), DMA((KC,)), DMA((KC,)),
         DMA((NY, NP)), DMA((NY, NP)), DMA((NY, NP)),
-        DMA((NY,)), DMA((NY,)), DMA((NZ,)), DMA((NZ,)), DMA((NY,)), DMA((NY,)), DMA((NH,)), DMA((NZH * NZ,)),
-        DMA((NX,)), DMA((NX,)), DMA((1,)), DMA((1,)), DMA((NX,)), DMA((NX,)),
+        DMA((NZ * NY,)), DMA((NZ * NY,)), DMA((NY,)), DMA((NY,)), DMA((NH,)), DMA((NZH * NZ,)),
+        DMA((KC, NX)), DMA((KC, NX)), DMA((KC,)), DMA((KC,)), DMA((KC, NX)), DMA((KC, NX)),
     ]
     return pl.pallas_call(
         functools.partial(kernel, dims, keys / 32.0),
@@ -361,11 +395,11 @@
             jax.ShapeDtypeStruct((rows, iheads), F32),
             jax.ShapeDtypeStruct((nk, idim), F32),
         ),
-        in_specs=[vm] * 6,
+        in_specs=[pl.BlockSpec(memory_space=pl.ANY)] * 6,
         out_specs=(vm, vm, vm),
         scratch_shapes=scratch,
         compiler_params=pltpu.CompilerParams(
-            collective_id=0, has_side_effects=True, vmem_limit_bytes=48 * 1024 * 1024
+            collective_id=0, has_side_effects=True, vmem_limit_bytes=56 * 1024 * 1024
         ),
         name="indexer_backward",
     )(q_attn, latent.T, lse_saved, q_index, k_index, head_weight)

time: 79.9 us -> 73.5 us (0.920)
  Pallas kernels: 71.8 us -> 67.6 us
  local copies, waits for them, and re-layouts: 6.99 us -> 4.4 us
    pallas_call x1, Pallas kernels: 71.8 us -> 67.6 us  [body(): pl.pallas_call(functools.partial(kernel, dims, keys / 32.0), out_shape=(j...]
    unnamed x15 -> x3, local copies, waits for them, and re-layouts: 6.99 us -> 4.4 us
where the time goes in v3:
time: 73.5 us; the launch traced here: 72.6 us
  Pallas kernels  67.6 us (92%)
  local copies, waits for them, and re-layouts  4.4 us (6%)
    pallas_call x1, Pallas kernels, body(): pl.pallas_call(functools.partial(kernel, dims, keys / 32.0), out_shape=(j...  67.6 us
    unnamed x3, local copies, waits for them, and re-layouts  4.4 us

profile of v3, /device:TPU:1, one launch (start us, length us, event | category | flops | bytes accessed | tf_op | source)
XLA Modules:
  0.0 72.6 jit_solution(7433251461427043205)
XLA Ops:
  0.6 67.6 %indexer_backward.1 = (f32[2,8,128]{2,1,0:T(8,128)}, f32[2,8]{1,0:T(2,128)}, f32[1024,128]{1,0:T(8,128)}) custom-call(bf16[2,16,576]{2,1,0:T(8,128)(2,1)} %q_hbm.1, bf16[576,1024]{1,0:T(8,128)(2,1)} %bitcast.1, f32[2,16]{1,0:T(2,128)} %lse_hbm.1, bf16[2,8,128]{2,1,0:T(8,128)(2,1)} %qi_hbm.1, bf16[1024,128]{1,0:T(8,128)(2,1)} %k_hbm.1, f32[2,8]{1,0:T(2,128)} %w_hbm.1), custom_call_target="tpu_custom_call" | custom-call | tf_op jit(solution)/shard_map/indexer_backward/pallas_call | solution.py:391
  68.2 1.3 %copy.12 = f32[2,8,128]{2,1,0:T(8,128)} copy(f32[2,8,128]{2,1,0:T(8,128)} %get-tuple-element.6) | data formatting | bytes 16384
  69.5 1.2 %copy.13 = f32[2,8]{1,0:T(2,128)} copy(f32[2,8]{1,0:T(2,128)} %get-tuple-element.7) | data formatting | bytes 128
  70.8 1.9 %copy.14 = f32[1024,128]{1,0:T(8,128)} copy(f32[1024,128]{1,0:T(8,128)} %get-tuple-element.8) | data formatting | bytes 1048576

commit v4 on v3

--- a/solution.py
+++ b/solution.py
@@ -12,6 +12,7 @@
 F32, BF16 = jnp.float32, jnp.bfloat16
 DIMS = (4, 8, 2, 4)
 KC = 2
+HC = 2
 NT = (((1,), (1,)), ((), ()))
 
 
@@ -38,7 +39,7 @@
     q_hbm, lat_hbm, lse_hbm, qi_hbm, k_hbm, w_hbm,
     gq_ref, gw_ref, gk_ref,
     q_ref, lse_ref, qi_ref, w_ref, s_in,
-    q_stage, i_stage, qbuf, ientry, ibuf, latbuf, kbuf, raw, wq, tacc, sacc, gbuf, masked,
+    q_stage, i_stage, qbuf, ientry, ibuf, latbuf, kbuf, keep, wq, tacc, sacc, gbuf, masked,
     st_buf, part, ry_buf, zsum, fq_buf,
     ck_send, ck_recv, gx_sum, gx_send, gx_recv, gz_send, gz_recv, ga_buf,
     s_eq, s_ei, r_eq, r_ei, s_core, r_core, s_ck, r_ck, s_up, s_down, r_y,
@@ -167,9 +168,6 @@
     krow = lax.broadcasted_iota(jnp.int32, (wide - width, nk), 0)
     for side in range(2):
         latbuf[side, width:] = jnp.where(krow < 3, -inv_scale, 0.0).astype(BF16)
-    for cp in loads[4:]:
-        cp.wait()
-
     pl.semaphore_wait(barrier, jnp.where(own_plane, n_greet - 2, n_greet))
 
     for r in (1 - zh, zh) if NZH == 2 else range(NZH):
@@ -184,10 +182,12 @@
                 send(*iargs)
                 send(*qargs)
     other = ctx_of(zl, y, 1 - c)
+    for cp in loads[4:]:
+        cp.wait()
     send(kbuf.at[0], kbuf.at[1], s_core.at[0], r_core.at[0], other, head)
     send(latbuf.at[0, :width], latbuf.at[1, :width], s_core.at[1], r_core.at[1], other, head)
 
-    NC = NH // 2
+    NC = NH // HC
     up, down = lax.rem(y + 1, NY), lax.rem(y + NY - 1, NY)
     far = NY // 2
     near = far - 1
@@ -195,7 +195,7 @@
     order.insert(NC // 2, NC)
 
     def piece(y0, n):
-        return ibuf.at[y0] if n is NC else qbuf.at[y0, pl.ds(2 * n, 2)]
+        return ibuf.at[y0] if n is NC else qbuf.at[y0, pl.ds(HC * n, HC)]
 
     def forward(y0, k, step, plus, minus):
         n = order[k]
@@ -213,8 +213,8 @@
                 arrived(ientry.at[h], r_ei.at[h])
             ibuf[y] = ientry[...].astype(F32)[:, :iheads, :].reshape(J, idim).astype(BF16)
         else:
-            for h in (2 * n, 2 * n + 1):
-                arrived(qbuf.at[y, h], r_eq.at[h])
+            for h in range(HC):
+                arrived(qbuf.at[y, HC * n + h], r_eq.at[HC * n + h])
         forward(y, k, 0, near > 0 or by_up(k), near > 0 or not by_up(k))
 
     CH = min(512, nk)
@@ -235,7 +235,7 @@
                 e = jnp.exp2(s * (scale * log2e))
                 tacc[y0, :, kcols] = jnp.sum(e.reshape(NH * heads // 8, 8, CH), axis=0)
                 rw = lax.dot_general(qi, kbuf[side, cols, :], NT, preferred_element_type=F32)
-                raw[y0, :, kcols] = rw
+                keep[y0, :, kcols] = jnp.where(rw > 0, 1.0, 0.0).astype(BF16)
                 sacc[y0, :, kcols] = jnp.sum((wcol * jnp.maximum(rw, 0.0)).reshape(J // 8, 8, CH), axis=0)
 
     arrived(kbuf.at[1], r_core.at[0])
@@ -281,7 +281,7 @@
     l = jnp.sum(jnp.where(at[1], mass, 0.0), axis=1, keepdims=True)
     t = jnp.sum(jnp.where(at[2], mass, 0.0), axis=1, keepdims=True)
     grad = factor * (jnp.exp(score - m) / l - target / t)
-    gbuf[...] = grad.astype(BF16).astype(F32)
+    gbuf[...] = grad
 
     nc = nk // KC
     nq = nc // NX
@@ -290,8 +290,9 @@
         cols = slice(q * nc, (q + 1) * nc)
         kcols = slice(side * nk + q * nc, side * nk + (q + 1) * nc)
         for y0 in range(NY):
-            g = jnp.where(raw[y0, :, kcols] > 0, gbuf[y0 : y0 + 1, kcols], 0.0)
-            masked[side, y0 * J : (y0 + 1) * J, cols] = g.astype(BF16)
+            g = jnp.broadcast_to(gbuf[y0 : y0 + 1, kcols], (16, nc)).astype(BF16)
+            g = keep[y0, :, kcols].reshape(J // 16, 16, nc) * g[None]
+            masked[side, y0 * J : (y0 + 1) * J, cols] = g.reshape(J, nc)
         return jnp.dot(wqt, masked[side, :, cols], preferred_element_type=F32)
 
     for q in range(KC):
@@ -367,7 +368,7 @@
     J = NH * iheads
     K2 = 2 * nk
     nq = nk // NX // KC
-    NP = NH // 2 + 1
+    NP = NH // HC + 1
     V, DMA = pltpu.VMEM, pltpu.SemaphoreType.DMA
     vm = pl.BlockSpec(memory_space=pltpu.VMEM)
     scratch = [
@@ -375,7 +376,7 @@
         V((rows, heads, wide), BF16), V((rows, heads, idim), BF16),
         V((NY, NH, heads, wide), BF16), V((NH, heads, idim), BF16), V((NY, J, idim), BF16),
         V((2, wide, nk), BF16), V((2, nk, idim), BF16),
-        V((NY, J, K2), F32), V((NY, J, idim), BF16),
+        V((NY, J, K2), BF16), V((NY, J, idim), BF16),
         V((NY, 8, K2), F32), V((NY, 8, K2), F32), V((NY, K2), F32), V((2, NY * J, nk), BF16),
         V((NZ * NY, 128), F32),
         V((NY, J, idim), BF16), V((NY, J, idim), BF16),
@@ -388,13 +389,14 @@
         DMA((NZ * NY,)), DMA((NZ * NY,)), DMA((NY,)), DMA((NY,)), DMA((NH,)), DMA((NZH * NZ,)),
         DMA((KC, NX)), DMA((KC, NX)), DMA((KC,)), DMA((KC,)), DMA((KC, NX)), DMA((KC, NX)),
     ]
-    return pl.pallas_call(
+    shapes = (
+        jax.ShapeDtypeStruct((rows, iheads, idim), F32),
+        jax.ShapeDtypeStruct((rows, iheads), F32),
+        jax.ShapeDtypeStruct((nk, idim), F32),
+    )
+    outs = pl.pallas_call(
         functools.partial(kernel, dims, keys / 32.0),
-        out_shape=(
-            jax.ShapeDtypeStruct((rows, iheads, idim), F32),
-            jax.ShapeDtypeStruct((rows, iheads), F32),
-            jax.ShapeDtypeStruct((nk, idim), F32),
-        ),
+        out_shape=shapes,
         in_specs=[pl.BlockSpec(memory_space=pl.ANY)] * 6,
         out_specs=(vm, vm, vm),
         scratch_shapes=scratch,
@@ -403,6 +405,26 @@
         ),
         name="indexer_backward",
     )(q_attn, latent.T, lse_saved, q_index, k_index, head_weight)
+    return pl.pallas_call(
+        store,
+        out_shape=shapes,
+        in_specs=[vm] * 3,
+        out_specs=tuple(pl.BlockSpec(memory_space=pl.ANY) for _ in shapes),
+        scratch_shapes=[DMA((3,))],
+        compiler_params=pltpu.CompilerParams(vmem_limit_bytes=58 * 1024 * 1024),
+        name="store_results",
+    )(*outs)
+
+
+def store(a_ref, b_ref, c_ref, a_out, b_out, c_out, sems):
+    copies = [
+        pltpu.make_async_copy(src, dst, sems.at[n])
+        for n, (src, dst) in enumerate(((a_ref, a_out), (b_ref, b_out), (c_ref, c_out)))
+    ]
+    for cp in copies:
+        cp.start()
+    for cp in copies:
+        cp.wait()
 
 
 def build(mesh, dims, keys):

time: 73.5 us -> 71.3 us (0.970)
  local copies, waits for them, and re-layouts: 4.4 us -> 0 us
  Pallas kernels: 67.6 us -> 70.5 us
    unnamed x3 -> x0, local copies, waits for them, and re-layouts: 4.4 us -> none
    pallas_call x1 -> x2, Pallas kernels: 67.6 us -> 70.5 us  [the longest x1 68.6 us: body(): pl.pallas_call(functools.partial(kernel, dims, keys / 32.0), out_shape=sh...]
where the time goes in v4:
time: 71.3 us; the launch traced here: 71.1 us
  Pallas kernels  70.5 us (99%)
    pallas_call x1, Pallas kernels, body(): pl.pallas_call(functools.partial(kernel, dims, keys / 32.0), out_shape=sh...  68.6 us
    pallas_call x1, Pallas kernels, body(): pl.pallas_call(store, out_shape=shapes, in_specs=[vm] * 3, out_specs=tupl...  1.89 us

profile of v4, /device:TPU:1, one launch (start us, length us, event | category | flops | bytes accessed | tf_op | source)
XLA Modules:
  0.0 71.1 jit_solution(13533108368857879636)
XLA Ops:
  0.6 68.6 %indexer_backward.1 = (f32[2,8,128]{2,1,0:T(8,128)}, f32[2,8]{1,0:T(2,128)}, f32[1024,128]{1,0:T(8,128)}) custom-call(bf16[2,16,576]{2,1,0:T(8,128)(2,1)} %q_hbm.1, bf16[576,1024]{1,0:T(8,128)(2,1)} %bitcast.1, f32[2,16]{1,0:T(2,128)} %lse_hbm.1, bf16[2,8,128]{2,1,0:T(8,128)(2,1)} %qi_hbm.1, bf16[1024,128]{1,0:T(8,128)(2,1)} %k_hbm.1, f32[2,8]{1,0:T(2,128)} %w_hbm.1), custom_call_target="tpu_custom_call" | custom-call | tf_op jit(solution)/shard_map/indexer_backward/pallas_call | solution.py:397
  69.3 1.9 %store_results.1 = (f32[2,8,128]{2,1,0:T(8,128)}, f32[2,8]{1,0:T(2,128)}, f32[1024,128]{1,0:T(8,128)}) custom-call(f32[2,8,128]{2,1,0:T(8,128)} %get-tuple-element.6.a_ref, f32[2,8]{1,0:T(2,128)} %get-tuple-element.7.b_ref, f32[1024,128]{1,0:T(8,128)} %get-tuple-element.8.c_ref), custom_call_target="tpu_custom_call" | custom-call | tf_op jit(solution)/shard_map/store_results/pallas_call | solution.py:408

commit v5 on v4

--- a/solution.py
+++ b/solution.py
@@ -16,12 +16,6 @@
 NT = (((1,), (1,)), ((), ()))
 
 
-def split3(v):
-    hi = v.astype(BF16).astype(F32)
-    mid = (v - hi).astype(BF16).astype(F32)
-    return hi, mid, v - hi - mid
-
-
 def column(row):
     n = row.shape[1]
     eye = lax.broadcasted_iota(jnp.int32, (n, n), 0) == lax.broadcasted_iota(jnp.int32, (n, n), 1)
@@ -37,12 +31,13 @@
 def kernel(
     dims, factor,
     q_hbm, lat_hbm, lse_hbm, qi_hbm, k_hbm, w_hbm,
-    gq_ref, gw_ref, gk_ref,
+    gq_hbm, gw_hbm, gk_hbm,
+    gq_ref, gw_ref, gk_ref, s_out,
     q_ref, lse_ref, qi_ref, w_ref, s_in,
-    q_stage, i_stage, qbuf, ientry, ibuf, latbuf, kbuf, keep, wq, tacc, sacc, gbuf, masked,
+    q_stage, a_stage, qbuf, abuf, latbuf, kbuf, keep, wq, tacc, sacc, gbuf, masked,
     st_buf, part, ry_buf, zsum, fq_buf,
     ck_send, ck_recv, gx_sum, gx_send, gx_recv, gz_send, gz_recv, ga_buf,
-    s_eq, s_ei, r_eq, r_ei, s_core, r_core, s_ck, r_ck, s_up, s_down, r_y,
+    s_eq, s_ea, r_eq, r_ea, s_core, r_core, s_ck, r_ck, s_up, s_down, r_y,
     s_st, r_st, s_ry, r_ry, s_fq, r_fq, s_gx, r_gx, s_gz, r_gz, s_ga, r_ga,
 ):
     NZ, NY, NZH, NX = dims
@@ -62,7 +57,6 @@
     base = wide - 128
     tail = width - base
     scale = width ** -0.5
-    inv_scale = width ** 0.5
     log2e = math.log2(math.e)
     own_plane = x == zl
 
@@ -110,16 +104,6 @@
         for dy in sorted(range(NY), key=lambda d: -min(d, NY - d)) for dz in range(NZ) if dy or dz
     ]
     hs = [lax.rem(head + d, NH) for d in range(NH)]
-
-    loads = [
-        pltpu.make_async_copy(src, dst, s_in.at[n])
-        for n, (src, dst) in enumerate((
-            (q_hbm, q_ref), (lse_hbm, lse_ref), (qi_hbm, qi_ref), (w_hbm, w_ref),
-            (k_hbm, kbuf.at[0]), (lat_hbm, latbuf.at[0, :width]),
-        ))
-    ]
-    for cp in loads:
-        cp.start()
 
     barrier = pltpu.get_barrier_semaphore()
 
@@ -141,6 +125,16 @@
                     greet(ctx_of(zl, y, c), r * NX + zl)
             else:
                 greet(ctx_of(z_, y, c), r * NX + zl)
+    loads = [
+        pltpu.make_async_copy(src, dst, s_in.at[n])
+        for n, (src, dst) in enumerate((
+            (q_hbm, q_ref), (lse_hbm, lse_ref), (qi_hbm, qi_ref), (w_hbm, w_ref),
+            (k_hbm, kbuf.at[0]), (lat_hbm, latbuf.at[0, :width]),
+        ))
+    ]
+    for cp in loads:
+        cp.start()
+
     greet(ctx_of(zl, y, 1 - c), head)
     for p in plane:
         greet(p[0], head)
@@ -153,33 +147,28 @@
         cp.wait()
     lane = lax.broadcasted_iota(jnp.int32, (heads, 128), 1)
     for r in range(rows):
-        t3 = list(split3(column(lse_ref[r : r + 1, :])))
-        w3 = [jnp.concatenate([v, jnp.zeros((heads - iheads, 1), F32)], axis=0)
-              for v in split3(column(w_ref[r : r + 1, :]))]
-        aug = jnp.zeros((heads, 128), F32)
-        for n, v in enumerate(t3 + w3):
-            aug = jnp.where(lane == tail + n, v, aug)
         q_stage[r, :, :base] = q_ref[r, :, :base]
         last = jnp.concatenate([q_ref[r, :, base:].astype(F32), jnp.zeros((heads, 128 - tail), F32)], axis=1)
-        q_stage[r, :, base:] = (last + aug).astype(BF16)
-        i_stage[r] = jnp.concatenate(
-            [qi_ref[r].astype(F32), jnp.zeros((heads - iheads, idim), F32)], axis=0
-        ).astype(BF16)
-    krow = lax.broadcasted_iota(jnp.int32, (wide - width, nk), 0)
+        qi = qi_ref[r].astype(F32)
+        qi = jnp.concatenate([pltpu.roll(qi, tail, 1), qi], axis=0)
+        q_stage[r, :, base:] = jnp.where(lane < tail, last, qi).astype(BF16)
+        a_stage[r : r + 1, :] = jnp.concatenate(
+            [lse_ref[r : r + 1, :], w_ref[r : r + 1, :], jnp.zeros((1, 128 - heads - iheads), F32)], axis=1
+        )
     for side in range(2):
-        latbuf[side, width:] = jnp.where(krow < 3, -inv_scale, 0.0).astype(BF16)
+        latbuf[side, width:] = jnp.zeros((wide - width, nk), BF16)
     pl.semaphore_wait(barrier, jnp.where(own_plane, n_greet - 2, n_greet))
 
     for r in (1 - zh, zh) if NZH == 2 else range(NZH):
         for d, z_ in enumerate(zls):
             to = (ctx_of(z_, y, c), r * NX + zl)
-            iargs = (i_stage.at[r], ientry.at[head], s_ei.at[r, d], r_ei.at[head], *to)
+            aargs = (a_stage.at[pl.ds(r, 1)], abuf.at[y, pl.ds(head, 1)], s_ea.at[r, d], r_ea.at[head], *to)
             qargs = (q_stage.at[r], qbuf.at[y, head], s_eq.at[r, d], r_eq.at[head], *to)
             if d == 0:
-                send_unless(own_plane & (zh == r), *iargs)
+                send_unless(own_plane & (zh == r), *aargs)
                 send_unless(own_plane & (zh == r), *qargs)
             else:
-                send(*iargs)
+                send(*aargs)
                 send(*qargs)
     other = ctx_of(zl, y, 1 - c)
     for cp in loads[4:]:
@@ -195,7 +184,7 @@
     order.insert(NC // 2, NC)
 
     def piece(y0, n):
-        return ibuf.at[y0] if n is NC else qbuf.at[y0, pl.ds(HC * n, HC)]
+        return abuf.at[y0] if n is NC else qbuf.at[y0, pl.ds(HC * n, HC)]
 
     def forward(y0, k, step, plus, minus):
         n = order[k]
@@ -210,8 +199,7 @@
     for k, n in enumerate(order):
         if n is NC:
             for h in range(NH):
-                arrived(ientry.at[h], r_ei.at[h])
-            ibuf[y] = ientry[...].astype(F32)[:, :iheads, :].reshape(J, idim).astype(BF16)
+                arrived(abuf.at[y, pl.ds(h, 1)], r_ea.at[h])
         else:
             for h in range(HC):
                 arrived(qbuf.at[y, HC * n + h], r_eq.at[HC * n + h])
@@ -221,18 +209,23 @@
 
     def block(y0):
         q = qbuf[y0].reshape(NH * heads, wide)
-        qi = ibuf[y0]
-        aug = qbuf[y0, :, :, base:].astype(F32).reshape(NH * heads, 128)
-        ln = lax.broadcasted_iota(jnp.int32, aug.shape, 1)
-        wide_col = jnp.sum(jnp.where((ln >= tail + 3) & (ln < tail + 6), aug, 0.0), axis=1, keepdims=True)
-        wcol = wide_col.reshape(NH, heads, 1)[:, :iheads, :].reshape(J, 1)
-        wq[y0] = (qi.astype(F32) * wcol).astype(BF16)
+        rest = qbuf[y0, :, :, base:].astype(F32)
+        low, high = rest[:, :iheads].reshape(J, 128), rest[:, iheads:].reshape(J, 128)
+        ln = lax.broadcasted_iota(jnp.int32, (J, 128), 1)
+        qi32 = jnp.where(ln < tail, pltpu.roll(low, 128 - tail, 1), high)
+        qi = qi32.astype(BF16)
+        aux = abuf[y0][:, None, :]
+        ln = lax.broadcasted_iota(jnp.int32, (NH, heads, 128), 2)
+        sub = lax.broadcasted_iota(jnp.int32, (NH, heads, 128), 1)
+        lse = jnp.sum(jnp.where(ln == sub, aux, 0.0), axis=2, keepdims=True).reshape(NH * heads, 1) * log2e
+        wcol = jnp.sum(jnp.where(ln == sub + heads, aux, 0.0)[:, :iheads], axis=2, keepdims=True).reshape(J, 1)
+        wq[y0] = (qi32 * wcol).astype(BF16)
         for side in range(2):
             for n in range(nk // CH):
                 cols = slice(n * CH, (n + 1) * CH)
                 kcols = slice(side * nk + n * CH, side * nk + (n + 1) * CH)
                 s = jnp.dot(q, latbuf[side, :, cols], preferred_element_type=F32)
-                e = jnp.exp2(s * (scale * log2e))
+                e = jnp.exp2(s * (scale * log2e) - lse)
                 tacc[y0, :, kcols] = jnp.sum(e.reshape(NH * heads // 8, 8, CH), axis=0)
                 rw = lax.dot_general(qi, kbuf[side, cols, :], NT, preferred_element_type=F32)
                 keep[y0, :, kcols] = jnp.where(rw > 0, 1.0, 0.0).astype(BF16)
@@ -349,11 +342,23 @@
         gq_ref[r] = own * column(w_ref[r : r + 1, :])
         gw_ref[r : r + 1, :] = row_of(jnp.sum(own * qi_ref[r].astype(F32), axis=1, keepdims=True))
 
+    stores = [
+        pltpu.make_async_copy(gq_ref, gq_hbm, s_out.at[KC]),
+        pltpu.make_async_copy(gw_ref, gw_hbm, s_out.at[KC + 1]),
+    ]
+    for cp in stores:
+        cp.start()
     for q in range(KC):
         for x_ in x_peers:
             arrived(ga_buf.at[q, x_], r_ga.at[q, x_])
-    gk_ref[...] = ga_buf[...].astype(F32).reshape(gk_ref.shape)
-
+        part_q = slice(q * nc, (q + 1) * nc)
+        gk_ref[part_q] = ga_buf[q].astype(F32).reshape(nc, idim)
+        cp = pltpu.make_async_copy(gk_ref.at[part_q], gk_hbm.at[part_q], s_out.at[q])
+        cp.start()
+        stores.append(cp)
+
+    for cp in stores:
+        cp.wait()
     for finish in sends:
         finish()
 
@@ -372,9 +377,10 @@
     V, DMA = pltpu.VMEM, pltpu.SemaphoreType.DMA
     vm = pl.BlockSpec(memory_space=pltpu.VMEM)
     scratch = [
+        V((rows, iheads, idim), F32), V((rows, iheads), F32), V((nk, idim), F32), DMA((KC + 2,)),
         V((rows, heads, width), BF16), V((rows, heads), F32), V((rows, iheads, idim), BF16), V((rows, iheads), F32), DMA((6,)),
-        V((rows, heads, wide), BF16), V((rows, heads, idim), BF16),
-        V((NY, NH, heads, wide), BF16), V((NH, heads, idim), BF16), V((NY, J, idim), BF16),
+        V((rows, heads, wide), BF16), V((rows, 128), F32),
+        V((NY, NH, heads, wide), BF16), V((NY, NH, 128), F32),
         V((2, wide, nk), BF16), V((2, nk, idim), BF16),
         V((NY, J, K2), BF16), V((NY, J, idim), BF16),
         V((NY, 8, K2), F32), V((NY, 8, K2), F32), V((NY, K2), F32), V((2, NY * J, nk), BF16),
@@ -398,7 +404,7 @@
         functools.partial(kernel, dims, keys / 32.0),
         out_shape=shapes,
         in_specs=[pl.BlockSpec(memory_space=pl.ANY)] * 6,
-        out_specs=(vm, vm, vm),
+        out_specs=tuple(pl.BlockSpec(memory_space=pl.ANY) for _ in shapes),
         scratch_shapes=scratch,
         compiler_params=pltpu.CompilerParams(
             collective_id=0, has_side_effects=True, vmem_limit_bytes=56 * 1024 * 1024

time: 71.3 us -> 69.6 us (0.976); the launches traced: 71.1 us -> 68.6 us
  Pallas kernels: 70.5 us -> 68 us
    pallas_call x1, Pallas kernels: 68.6 us -> 66.1 us  [body(): pl.pallas_call(functools.partial(kernel, dims, keys / 32.0), out_shape=sh...]
where the time goes in v5:
time: 69.6 us; the launch traced here: 68.6 us
  Pallas kernels  68 us (98%)
    pallas_call x1, Pallas kernels, body(): pl.pallas_call(functools.partial(kernel, dims, keys / 32.0), out_shape=sh...  66.1 us
    pallas_call x1, Pallas kernels, body(): pl.pallas_call(store, out_shape=shapes, in_specs=[vm] * 3, out_specs=tupl...  1.89 us

profile of v5, /device:TPU:1, one launch (start us, length us, event | category | flops | bytes accessed | tf_op | source)
XLA Modules:
  0.0 68.6 jit_solution(9673531757145292884)
XLA Ops:
  0.6 66.1 %indexer_backward.1 = (f32[2,8,128]{2,1,0:T(8,128)}, f32[2,8]{1,0:T(2,128)}, f32[1024,128]{1,0:T(8,128)}) custom-call(bf16[2,16,576]{2,1,0:T(8,128)(2,1)} %q_hbm.1, bf16[576,1024]{1,0:T(8,128)(2,1)} %bitcast.1, f32[2,16]{1,0:T(2,128)} %lse_hbm.1, bf16[2,8,128]{2,1,0:T(8,128)(2,1)} %qi_hbm.1, bf16[1024,128]{1,0:T(8,128)(2,1)} %k_hbm.1, f32[2,8]{1,0:T(2,128)} %w_hbm.1), custom_call_target="tpu_custom_call" | custom-call | tf_op jit(solution)/shard_map/indexer_backward/pallas_call | solution.py:403
  66.7 1.9 %store_results.1 = (f32[2,8,128]{2,1,0:T(8,128)}, f32[2,8]{1,0:T(2,128)}, f32[1024,128]{1,0:T(8,128)}) custom-call(f32[2,8,128]{2,1,0:T(8,128)} %get-tuple-element.6.a_ref, f32[2,8]{1,0:T(2,128)} %get-tuple-element.7.b_ref, f32[1024,128]{1,0:T(8,128)} %get-tuple-element.8.c_ref), custom_call_target="tpu_custom_call" | custom-call | tf_op jit(solution)/shard_map/store_results/pallas_call | solution.py:414

commit v6 on v5

--- a/solution.py
+++ b/solution.py
@@ -12,7 +12,6 @@
 F32, BF16 = jnp.float32, jnp.bfloat16
 DIMS = (4, 8, 2, 4)
 KC = 2
-HC = 2
 NT = (((1,), (1,)), ((), ()))
 
 
@@ -34,7 +33,7 @@
     gq_hbm, gw_hbm, gk_hbm,
     gq_ref, gw_ref, gk_ref, s_out,
     q_ref, lse_ref, qi_ref, w_ref, s_in,
-    q_stage, a_stage, qbuf, abuf, latbuf, kbuf, keep, wq, tacc, sacc, gbuf, masked,
+    q_stage, a_stage, qbuf, abuf, latbuf, kbuf, keep, wq, target, score, local, gbuf, masked,
     st_buf, part, ry_buf, zsum, fq_buf,
     ck_send, ck_recv, gx_sum, gx_send, gx_recv, gz_send, gz_recv, ga_buf,
     s_eq, s_ea, r_eq, r_ea, s_core, r_core, s_ck, r_ck, s_up, s_down, r_y,
@@ -79,6 +78,11 @@
         cp.start()
         sends.append(cp.wait_send)
 
+    def drain(count):
+        for finish in sends[:count]:
+            finish()
+        del sends[:count]
+
     def send_unless(local, src, dst, ssem, rsem, ctx_, head_):
         @pl.when(jnp.logical_not(local))
         def _():
@@ -97,7 +101,7 @@
 
     y_peers = [lax.rem(y + d, NY) for d in range(1, NY)]
     z_peers = [lax.rem(zl + d, NZ) for d in range(1, NZ)]
-    x_peers = [lax.rem(x + d, NX) for d in range(1, NX)]
+    x_peers = [lax.rem(x + d, NX) for d in sorted(range(1, NX), key=lambda d: -min(d, NX - d))]
     zls = [zl] + z_peers
     plane = [
         (ctx_of(lax.rem(zl + dz, NZ), lax.rem(y + dy, NY), c), lax.rem(zl + dz, NZ) * NY + lax.rem(y + dy, NY))
@@ -176,15 +180,18 @@
     send(kbuf.at[0], kbuf.at[1], s_core.at[0], r_core.at[0], other, head)
     send(latbuf.at[0, :width], latbuf.at[1, :width], s_core.at[1], r_core.at[1], other, head)
 
-    NC = NH // HC
+    NC = NH
     up, down = lax.rem(y + 1, NY), lax.rem(y + NY - 1, NY)
     far = NY // 2
     near = far - 1
-    order = [lax.rem(zh * (NC // 2) + n, NC) for n in range(NC)]
+    order = [
+        lax.rem(zh + dz, NZH) * NX + lax.rem(x + dx, NX)
+        for dz in range(NZH) for dx in sorted(range(NX), key=lambda d: min(d, NX - d))
+    ]
     order.insert(NC // 2, NC)
 
     def piece(y0, n):
-        return abuf.at[y0] if n is NC else qbuf.at[y0, pl.ds(HC * n, HC)]
+        return abuf.at[y0] if n is NC else qbuf.at[y0, n]
 
     def forward(y0, k, step, plus, minus):
         n = order[k]
@@ -201,8 +208,7 @@
             for h in range(NH):
                 arrived(abuf.at[y, pl.ds(h, 1)], r_ea.at[h])
         else:
-            for h in range(HC):
-                arrived(qbuf.at[y, HC * n + h], r_eq.at[HC * n + h])
+            arrived(qbuf.at[y, n], r_eq.at[n])
         forward(y, k, 0, near > 0 or by_up(k), near > 0 or not by_up(k))
 
     CH = min(512, nk)
@@ -226,10 +232,16 @@
                 kcols = slice(side * nk + n * CH, side * nk + (n + 1) * CH)
                 s = jnp.dot(q, latbuf[side, :, cols], preferred_element_type=F32)
                 e = jnp.exp2(s * (scale * log2e) - lse)
-                tacc[y0, :, kcols] = jnp.sum(e.reshape(NH * heads // 8, 8, CH), axis=0)
+                target[pl.ds(y0, 1), kcols] = jnp.sum(e, axis=0, keepdims=True)
                 rw = lax.dot_general(qi, kbuf[side, cols, :], NT, preferred_element_type=F32)
                 keep[y0, :, kcols] = jnp.where(rw > 0, 1.0, 0.0).astype(BF16)
-                sacc[y0, :, kcols] = jnp.sum((wcol * jnp.maximum(rw, 0.0)).reshape(J // 8, 8, CH), axis=0)
+                score[pl.ds(y0, 1), kcols] = jnp.sum(wcol * jnp.maximum(rw, 0.0), axis=0, keepdims=True)
+        srow = score[pl.ds(y0, 1), :]
+        m = jnp.max(srow, axis=1, keepdims=True)
+        l = jnp.sum(jnp.exp(srow - m), axis=1, keepdims=True)
+        t = jnp.sum(target[pl.ds(y0, 1), :], axis=1, keepdims=True)
+        ln = lax.broadcasted_iota(jnp.int32, (1, 128), 1)
+        local[pl.ds(y0, 1), :] = jnp.where(ln == 0, m, jnp.where(ln == 1, l, t))
 
     arrived(kbuf.at[1], r_core.at[0])
     arrived(latbuf.at[1, :width], r_core.at[1])
@@ -249,20 +261,18 @@
         arrived(piece(yf, n), r_y.at[yf, n])
     block(yf)
 
-    target = jnp.sum(tacc[...], axis=1)
-    score = jnp.sum(sacc[...], axis=1)
-    m = jnp.max(score, axis=1, keepdims=True)
-    l = jnp.sum(jnp.exp(score - m), axis=1, keepdims=True)
-    t = jnp.sum(target, axis=1, keepdims=True)
+    m, l, t = (local[:, n : n + 1] for n in range(3))
     sl = lax.broadcasted_iota(jnp.int32, (NY, 128), 1)
     ss = lax.broadcasted_iota(jnp.int32, (NY, 128), 0)
     at = [sl == ss + n * NY for n in range(3)]
     me = zl * NY + y
     mine = jnp.where(at[0], m, jnp.where(at[1], l, jnp.where(at[2], t, 0.0)))
     st_buf[pl.ds(me, 1), :] = jnp.sum(mine, axis=0, keepdims=True)
+    before = len(sends)
     for n, (dev, _) in enumerate(plane):
         send(st_buf.at[pl.ds(me, 1)], st_buf.at[pl.ds(me, 1)], s_st.at[n], r_st.at[me], dev, head)
     wqt = wq[...].reshape(NY * J, idim).astype(F32).T.astype(BF16)
+    drain(before)
     for _, slot in plane:
         arrived(st_buf.at[pl.ds(slot, 1)], r_st.at[slot])
     stats = st_buf[...]
@@ -273,7 +283,7 @@
     m = jnp.sum(jnp.where(at[1], top, 0.0), axis=1, keepdims=True)
     l = jnp.sum(jnp.where(at[1], mass, 0.0), axis=1, keepdims=True)
     t = jnp.sum(jnp.where(at[2], mass, 0.0), axis=1, keepdims=True)
-    grad = factor * (jnp.exp(score - m) / l - target / t)
+    grad = factor * (jnp.exp(score[...] - m) / l - target[...] / t)
     gbuf[...] = grad
 
     nc = nk // KC
@@ -308,6 +318,8 @@
     for n, y_ in enumerate(y_peers):
         send(part.at[y_], ry_buf.at[y], s_ry.at[n], r_ry.at[y], ctx_of(zl, y_, c), head)
 
+    drain(len(sends) - len(y_peers) - KC * len(x_peers))
+
     for q in range(KC):
         gsum = gx_sum[q, x]
         for x_ in x_peers:
@@ -328,6 +340,8 @@
             send_unless(own_plane, *args)
         else:
             send(*args)
+
+    drain(len(sends) - NH - KC)
 
     for q in range(KC):
         arrived(gz_recv.at[q], r_gz.at[q])
@@ -359,8 +373,7 @@
 
     for cp in stores:
         cp.wait()
-    for finish in sends:
-        finish()
+    drain(len(sends))
 
 
 def body(dims, keys, q_attn, latent, lse_saved, q_index, k_index, head_weight):
@@ -373,7 +386,7 @@
     J = NH * iheads
     K2 = 2 * nk
     nq = nk // NX // KC
-    NP = NH // HC + 1
+    NP = NH + 1
     V, DMA = pltpu.VMEM, pltpu.SemaphoreType.DMA
     vm = pl.BlockSpec(memory_space=pltpu.VMEM)
     scratch = [
@@ -383,7 +396,7 @@
         V((NY, NH, heads, wide), BF16), V((NY, NH, 128), F32),
         V((2, wide, nk), BF16), V((2, nk, idim), BF16),
         V((NY, J, K2), BF16), V((NY, J, idim), BF16),
-        V((NY, 8, K2), F32), V((NY, 8, K2), F32), V((NY, K2), F32), V((2, NY * J, nk), BF16),
+        V((NY, K2), F32), V((NY, K2), F32), V((NY, 128), F32), V((NY, K2), F32), V((2, NY * J, nk), BF16),
         V((NZ * NY, 128), F32),
         V((NY, J, idim), BF16), V((NY, J, idim), BF16),
         V((NH, iheads, idim), F32), V((NZH * NZ, iheads, idim), F32),
@@ -416,17 +429,17 @@
         out_shape=shapes,
         in_specs=[vm] * 3,
         out_specs=tuple(pl.BlockSpec(memory_space=pl.ANY) for _ in shapes),
-        scratch_shapes=[DMA((3,))],
+        scratch_shapes=[DMA((10,))],
         compiler_params=pltpu.CompilerParams(vmem_limit_bytes=58 * 1024 * 1024),
         name="store_results",
     )(*outs)
 
 
 def store(a_ref, b_ref, c_ref, a_out, b_out, c_out, sems):
-    copies = [
-        pltpu.make_async_copy(src, dst, sems.at[n])
-        for n, (src, dst) in enumerate(((a_ref, a_out), (b_ref, b_out), (c_ref, c_out)))
-    ]
+    n = c_ref.shape[0] // 8
+    pairs = [(c_ref.at[pl.ds(i * n, n)], c_out.at[pl.ds(i * n, n)]) for i in range(8)]
+    pairs += [(a_ref, a_out), (b_ref, b_out)]
+    copies = [pltpu.make_async_copy(src, dst, sems.at[i]) for i, (src, dst) in enumerate(pairs)]
     for cp in copies:
         cp.start()
     for cp in copies:

time: 69.6 us -> 69.3 us (level); the launches traced: 68.6 us -> 69.1 us
  no operation moved by 1% of the time
where the time goes in v6:
time: 69.3 us; the launch traced here: 69.1 us
  Pallas kernels  68.5 us (99%)
    pallas_call x1, Pallas kernels, body(): pl.pallas_call(functools.partial(kernel, dims, keys / 32.0), out_shape=sh...  66.5 us
    pallas_call x1, Pallas kernels, body(): pl.pallas_call(store, out_shape=shapes, in_specs=[vm] * 3, out_specs=tupl...  1.93 us

profile of v6, /device:TPU:1, one launch (start us, length us, event | category | flops | bytes accessed | tf_op | source)
XLA Modules:
  0.0 69.1 jit_solution(4952325758151488117)
XLA Ops:
  0.6 66.5 %indexer_backward.1 = (f32[2,8,128]{2,1,0:T(8,128)}, f32[2,8]{1,0:T(2,128)}, f32[1024,128]{1,0:T(8,128)}) custom-call(bf16[2,16,576]{2,1,0:T(8,128)(2,1)} %q_hbm.1, bf16[576,1024]{1,0:T(8,128)(2,1)} %bitcast.1, f32[2,16]{1,0:T(2,128)} %lse_hbm.1, bf16[2,8,128]{2,1,0:T(8,128)(2,1)} %qi_hbm.1, bf16[1024,128]{1,0:T(8,128)(2,1)} %k_hbm.1, f32[2,8]{1,0:T(2,128)} %w_hbm.1), custom_call_target="tpu_custom_call" | custom-call | tf_op jit(solution)/shard_map/indexer_backward/pallas_call | solution.py:416
  67.2 1.9 %store_results.1 = (f32[2,8,128]{2,1,0:T(8,128)}, f32[2,8]{1,0:T(2,128)}, f32[1024,128]{1,0:T(8,128)}) custom-call(f32[2,8,128]{2,1,0:T(8,128)} %get-tuple-element.6.a_ref, f32[2,8]{1,0:T(2,128)} %get-tuple-element.7.b_ref, f32[1024,128]{1,0:T(8,128)} %get-tuple-element.8.c_ref), custom_call_target="tpu_custom_call" | custom-call | tf_op jit(solution)/shard_map/store_results/pallas_call | solution.py:427

commit v7 on v6

--- a/solution.py
+++ b/solution.py
@@ -12,7 +12,6 @@
 F32, BF16 = jnp.float32, jnp.bfloat16
 DIMS = (4, 8, 2, 4)
 KC = 2
-NT = (((1,), (1,)), ((), ()))
 
 
 def column(row):
@@ -33,7 +32,7 @@
     gq_hbm, gw_hbm, gk_hbm,
     gq_ref, gw_ref, gk_ref, s_out,
     q_ref, lse_ref, qi_ref, w_ref, s_in,
-    q_stage, a_stage, qbuf, abuf, latbuf, kbuf, keep, wq, target, score, local, gbuf, masked,
+    q_stage, a_stage, qbuf, abuf, latbuf, kbuf, ktbuf, keep, wq, target, score, local, masked,
     st_buf, part, ry_buf, zsum, fq_buf,
     ck_send, ck_recv, gx_sum, gx_send, gx_recv, gz_send, gz_recv, ga_buf,
     s_eq, s_ea, r_eq, r_ea, s_core, r_core, s_ck, r_ck, s_up, s_down, r_y,
@@ -180,6 +179,8 @@
     send(kbuf.at[0], kbuf.at[1], s_core.at[0], r_core.at[0], other, head)
     send(latbuf.at[0, :width], latbuf.at[1, :width], s_core.at[1], r_core.at[1], other, head)
 
+    ktbuf[0] = kbuf[0].astype(F32).T.astype(BF16)
+
     NC = NH
     up, down = lax.rem(y + 1, NY), lax.rem(y + NY - 1, NY)
     far = NY // 2
@@ -233,17 +234,20 @@
                 s = jnp.dot(q, latbuf[side, :, cols], preferred_element_type=F32)
                 e = jnp.exp2(s * (scale * log2e) - lse)
                 target[pl.ds(y0, 1), kcols] = jnp.sum(e, axis=0, keepdims=True)
-                rw = lax.dot_general(qi, kbuf[side, cols, :], NT, preferred_element_type=F32)
+                rw = jnp.dot(qi, ktbuf[side, :, cols], preferred_element_type=F32)
                 keep[y0, :, kcols] = jnp.where(rw > 0, 1.0, 0.0).astype(BF16)
                 score[pl.ds(y0, 1), kcols] = jnp.sum(wcol * jnp.maximum(rw, 0.0), axis=0, keepdims=True)
         srow = score[pl.ds(y0, 1), :]
         m = jnp.max(srow, axis=1, keepdims=True)
-        l = jnp.sum(jnp.exp(srow - m), axis=1, keepdims=True)
+        erow = jnp.exp(srow - m)
+        score[pl.ds(y0, 1), :] = erow
+        l = jnp.sum(erow, axis=1, keepdims=True)
         t = jnp.sum(target[pl.ds(y0, 1), :], axis=1, keepdims=True)
         ln = lax.broadcasted_iota(jnp.int32, (1, 128), 1)
         local[pl.ds(y0, 1), :] = jnp.where(ln == 0, m, jnp.where(ln == 1, l, t))
 
     arrived(kbuf.at[1], r_core.at[0])
+    ktbuf[1] = kbuf[1].astype(F32).T.astype(BF16)
     arrived(latbuf.at[1, :width], r_core.at[1])
     block(y)
     for step in range(1, near + 1):
@@ -262,6 +266,7 @@
     block(yf)
 
     m, l, t = (local[:, n : n + 1] for n in range(3))
+    m_local = m
     sl = lax.broadcasted_iota(jnp.int32, (NY, 128), 1)
     ss = lax.broadcasted_iota(jnp.int32, (NY, 128), 0)
     at = [sl == ss + n * NY for n in range(3)]
@@ -283,8 +288,8 @@
     m = jnp.sum(jnp.where(at[1], top, 0.0), axis=1, keepdims=True)
     l = jnp.sum(jnp.where(at[1], mass, 0.0), axis=1, keepdims=True)
     t = jnp.sum(jnp.where(at[2], mass, 0.0), axis=1, keepdims=True)
-    grad = factor * (jnp.exp(score[...] - m) / l - target[...] / t)
-    gbuf[...] = grad
+    on_soft = jnp.exp(m_local - m) / l
+    on_target = 1.0 / t
 
     nc = nk // KC
     nq = nc // NX
@@ -292,8 +297,9 @@
     def mask(side, q):
         cols = slice(q * nc, (q + 1) * nc)
         kcols = slice(side * nk + q * nc, side * nk + (q + 1) * nc)
+        grad = factor * (score[:, kcols] * on_soft - target[:, kcols] * on_target)
         for y0 in range(NY):
-            g = jnp.broadcast_to(gbuf[y0 : y0 + 1, kcols], (16, nc)).astype(BF16)
+            g = jnp.broadcast_to(grad[y0 : y0 + 1], (16, nc)).astype(BF16)
             g = keep[y0, :, kcols].reshape(J // 16, 16, nc) * g[None]
             masked[side, y0 * J : (y0 + 1) * J, cols] = g.reshape(J, nc)
         return jnp.dot(wqt, masked[side, :, cols], preferred_element_type=F32)
@@ -394,9 +400,9 @@
         V((rows, heads, width), BF16), V((rows, heads), F32), V((rows, iheads, idim), BF16), V((rows, iheads), F32), DMA((6,)),
         V((rows, heads, wide), BF16), V((rows, 128), F32),
         V((NY, NH, heads, wide), BF16), V((NY, NH, 128), F32),
-        V((2, wide, nk), BF16), V((2, nk, idim), BF16),
+        V((2, wide, nk), BF16), V((2, nk, idim), BF16), V((2, idim, nk), BF16),
         V((NY, J, K2), BF16), V((NY, J, idim), BF16),
-        V((NY, K2), F32), V((NY, K2), F32), V((NY, 128), F32), V((NY, K2), F32), V((2, NY * J, nk), BF16),
+        V((NY, K2), F32), V((NY, K2), F32), V((NY, 128), F32), V((2, NY * J, nk), BF16),
         V((NZ * NY, 128), F32),
         V((NY, J, idim), BF16), V((NY, J, idim), BF16),
         V((NH, iheads, idim), F32), V((NZH * NZ, iheads, idim), F32),

time: 69.3 us -> 69.7 us (level)
  no operation moved by 1% of the time
where the time goes in v7:
time: 69.7 us; the launch traced here: 69.5 us
  Pallas kernels  68.9 us (99%)
    pallas_call x1, Pallas kernels, body(): pl.pallas_call(functools.partial(kernel, dims, keys / 32.0), out_shape=sh...  66.9 us
    pallas_call x1, Pallas kernels, body(): pl.pallas_call(store, out_shape=shapes, in_specs=[vm] * 3, out_specs=tupl...  1.93 us

profile of v7, /device:TPU:1, one launch (start us, length us, event | category | flops | bytes accessed | tf_op | source)
XLA Modules:
  0.0 69.5 jit_solution(3693865029673751470)
XLA Ops:
  0.6 66.9 %indexer_backward.1 = (f32[2,8,128]{2,1,0:T(8,128)}, f32[2,8]{1,0:T(2,128)}, f32[1024,128]{1,0:T(8,128)}) custom-call(bf16[2,16,576]{2,1,0:T(8,128)(2,1)} %q_hbm.1, bf16[576,1024]{1,0:T(8,128)(2,1)} %bitcast.1, f32[2,16]{1,0:T(2,128)} %lse_hbm.1, bf16[2,8,128]{2,1,0:T(8,128)(2,1)} %qi_hbm.1, bf16[1024,128]{1,0:T(8,128)(2,1)} %k_hbm.1, f32[2,8]{1,0:T(2,128)} %w_hbm.1), custom_call_target="tpu_custom_call" | custom-call | tf_op jit(solution)/shard_map/indexer_backward/pallas_call | solution.py:422
  67.6 1.9 %store_results.1 = (f32[2,8,128]{2,1,0:T(8,128)}, f32[2,8]{1,0:T(2,128)}, f32[1024,128]{1,0:T(8,128)}) custom-call(f32[2,8,128]{2,1,0:T(8,128)} %get-tuple-element.6.a_ref, f32[2,8]{1,0:T(2,128)} %get-tuple-element.7.b_ref, f32[1024,128]{1,0:T(8,128)} %get-tuple-element.8.c_ref), custom_call_target="tpu_custom_call" | custom-call | tf_op jit(solution)/shard_map/store_results/pallas_call | solution.py:433

commit v8 on v6

--- a/solution.py
+++ b/solution.py
@@ -200,16 +200,39 @@
         if minus:
             send(piece(y0, n), piece(y0, n), s_down.at[step, k], r_y.at[y0, n], ctx_of(zl, down, c), head)
 
+    first, second = range(NC // 2), range(NC // 2, NC + 1)
+
     def by_up(k):
-        return k <= NC // 2
-
-    for k, n in enumerate(order):
-        if n is NC:
-            for h in range(NH):
-                arrived(abuf.at[y, pl.ds(h, 1)], r_ea.at[h])
+        return (k if k in first else k - second[0]) % 2 == 0
+
+    def take(step, k):
+        n = order[k]
+        if step == 0:
+            if n is NC:
+                for h in range(NH):
+                    arrived(abuf.at[y, pl.ds(h, 1)], r_ea.at[h])
+            else:
+                arrived(qbuf.at[y, n], r_eq.at[n])
+            forward(y, k, 0, near > 0 or by_up(k), near > 0 or not by_up(k))
+        elif step <= near:
+            yu, yd = lax.rem(y + NY - step, NY), lax.rem(y + step, NY)
+            arrived(piece(yu, n), r_y.at[yu, n])
+            forward(yu, k, step, step < near or by_up(k), False)
+            arrived(piece(yd, n), r_y.at[yd, n])
+            forward(yd, k, step, False, step < near or not by_up(k))
         else:
-            arrived(qbuf.at[y, n], r_eq.at[n])
-        forward(y, k, 0, near > 0 or by_up(k), near > 0 or not by_up(k))
+            yf = lax.rem(y + far, NY)
+            arrived(piece(yf, n), r_y.at[yf, n])
+
+    def stage(step):
+        ahead = [(step, k) for k in first] if step <= far else []
+        behind = [(step - 1, k) for k in second] if step > 0 else []
+        for n in range(max(len(ahead), len(behind))):
+            for s_, k in ahead[n : n + 1] + behind[n : n + 1]:
+                take(s_, k)
+
+    stage(0)
+    stage(1)
 
     CH = min(512, nk)
 
@@ -247,19 +270,11 @@
     arrived(latbuf.at[1, :width], r_core.at[1])
     block(y)
     for step in range(1, near + 1):
-        yu = lax.rem(y + NY - step, NY)
-        yd = lax.rem(y + step, NY)
-        for k, n in enumerate(order):
-            arrived(piece(yu, n), r_y.at[yu, n])
-            forward(yu, k, step, step < near or by_up(k), False)
-            arrived(piece(yd, n), r_y.at[yd, n])
-            forward(yd, k, step, False, step < near or not by_up(k))
-        block(yu)
-        block(yd)
-    yf = lax.rem(y + far, NY)
-    for n in order:
-        arrived(piece(yf, n), r_y.at[yf, n])
-    block(yf)
+        stage(step + 1)
+        block(lax.rem(y + NY - step, NY))
+        block(lax.rem(y + step, NY))
+    stage(far + 1)
+    block(lax.rem(y + far, NY))
 
     m, l, t = (local[:, n : n + 1] for n in range(3))
     sl = lax.broadcasted_iota(jnp.int32, (NY, 128), 1)

time: 69.3 us -> 71.1 us (1.026)
  Pallas kernels: 68.5 us -> 70.3 us
    pallas_call x1, Pallas kernels: 66.5 us -> 68.3 us  [body(): pl.pallas_call(functools.partial(kernel, dims, keys / 32.0), out_shape=sh...]
where the time goes in v8:
time: 71.1 us; the launch traced here: 70.9 us
  Pallas kernels  70.3 us (99%)
    pallas_call x1, Pallas kernels, body(): pl.pallas_call(functools.partial(kernel, dims, keys / 32.0), out_shape=sh...  68.3 us
    pallas_call x1, Pallas kernels, body(): pl.pallas_call(store, out_shape=shapes, in_specs=[vm] * 3, out_specs=tupl...  1.93 us

profile of v8, /device:TPU:1, one launch (start us, length us, event | category | flops | bytes accessed | tf_op | source)
XLA Modules:
  0.0 70.9 jit_solution(10351913579861383602)
XLA Ops:
  0.6 68.3 %indexer_backward.1 = (f32[2,8,128]{2,1,0:T(8,128)}, f32[2,8]{1,0:T(2,128)}, f32[1024,128]{1,0:T(8,128)}) custom-call(bf16[2,16,576]{2,1,0:T(8,128)(2,1)} %q_hbm.1, bf16[576,1024]{1,0:T(8,128)(2,1)} %bitcast.1, f32[2,16]{1,0:T(2,128)} %lse_hbm.1, bf16[2,8,128]{2,1,0:T(8,128)(2,1)} %qi_hbm.1, bf16[1024,128]{1,0:T(8,128)(2,1)} %k_hbm.1, f32[2,8]{1,0:T(2,128)} %w_hbm.1), custom_call_target="tpu_custom_call" | custom-call | tf_op jit(solution)/shard_map/indexer_backward/pallas_call | solution.py:431
  69.0 1.9 %store_results.1 = (f32[2,8,128]{2,1,0:T(8,128)}, f32[2,8]{1,0:T(2,128)}, f32[1024,128]{1,0:T(8,128)}) custom-call(f32[2,8,128]{2,1,0:T(8,128)} %get-tuple-element.6.a_ref, f32[2,8]{1,0:T(2,128)} %get-tuple-element.7.b_ref, f32[1024,128]{1,0:T(8,128)} %get-tuple-element.8.c_ref), custom_call_target="tpu_custom_call" | custom-call | tf_op jit(solution)/shard_map/store_results/pallas_call | solution.py:442

commit v9 on v7

--- a/solution.py
+++ b/solution.py
@@ -12,6 +12,7 @@
 F32, BF16 = jnp.float32, jnp.bfloat16
 DIMS = (4, 8, 2, 4)
 KC = 2
+NT = (((1,), (1,)), ((), ()))
 
 
 def column(row):
@@ -32,7 +33,7 @@
     gq_hbm, gw_hbm, gk_hbm,
     gq_ref, gw_ref, gk_ref, s_out,
     q_ref, lse_ref, qi_ref, w_ref, s_in,
-    q_stage, a_stage, qbuf, abuf, latbuf, kbuf, ktbuf, keep, wq, target, score, local, masked,
+    q_stage, a_stage, qbuf, abuf, latbuf, kbuf, keep, wq, target, score, local, masked,
     st_buf, part, ry_buf, zsum, fq_buf,
     ck_send, ck_recv, gx_sum, gx_send, gx_recv, gz_send, gz_recv, ga_buf,
     s_eq, s_ea, r_eq, r_ea, s_core, r_core, s_ck, r_ck, s_up, s_down, r_y,
@@ -162,7 +163,7 @@
         latbuf[side, width:] = jnp.zeros((wide - width, nk), BF16)
     pl.semaphore_wait(barrier, jnp.where(own_plane, n_greet - 2, n_greet))
 
-    for r in (1 - zh, zh) if NZH == 2 else range(NZH):
+    for r in (zh, 1 - zh) if NZH == 2 else range(NZH):
         for d, z_ in enumerate(zls):
             to = (ctx_of(z_, y, c), r * NX + zl)
             aargs = (a_stage.at[pl.ds(r, 1)], abuf.at[y, pl.ds(head, 1)], s_ea.at[r, d], r_ea.at[head], *to)
@@ -178,8 +179,6 @@
         cp.wait()
     send(kbuf.at[0], kbuf.at[1], s_core.at[0], r_core.at[0], other, head)
     send(latbuf.at[0, :width], latbuf.at[1, :width], s_core.at[1], r_core.at[1], other, head)
-
-    ktbuf[0] = kbuf[0].astype(F32).T.astype(BF16)
 
     NC = NH
     up, down = lax.rem(y + 1, NY), lax.rem(y + NY - 1, NY)
@@ -234,7 +233,7 @@
                 s = jnp.dot(q, latbuf[side, :, cols], preferred_element_type=F32)
                 e = jnp.exp2(s * (scale * log2e) - lse)
                 target[pl.ds(y0, 1), kcols] = jnp.sum(e, axis=0, keepdims=True)
-                rw = jnp.dot(qi, ktbuf[side, :, cols], preferred_element_type=F32)
+                rw = lax.dot_general(qi, kbuf[side, cols, :], NT, preferred_element_type=F32)
                 keep[y0, :, kcols] = jnp.where(rw > 0, 1.0, 0.0).astype(BF16)
                 score[pl.ds(y0, 1), kcols] = jnp.sum(wcol * jnp.maximum(rw, 0.0), axis=0, keepdims=True)
         srow = score[pl.ds(y0, 1), :]
@@ -247,7 +246,6 @@
         local[pl.ds(y0, 1), :] = jnp.where(ln == 0, m, jnp.where(ln == 1, l, t))
 
     arrived(kbuf.at[1], r_core.at[0])
-    ktbuf[1] = kbuf[1].astype(F32).T.astype(BF16)
     arrived(latbuf.at[1, :width], r_core.at[1])
     block(y)
     for step in range(1, near + 1):
@@ -400,7 +398,7 @@
         V((rows, heads, width), BF16), V((rows, heads), F32), V((rows, iheads, idim), BF16), V((rows, iheads), F32), DMA((6,)),
         V((rows, heads, wide), BF16), V((rows, 128), F32),
         V((NY, NH, heads, wide), BF16), V((NY, NH, 128), F32),
-        V((2, wide, nk), BF16), V((2, nk, idim), BF16), V((2, idim, nk), BF16),
+        V((2, wide, nk), BF16), V((2, nk, idim), BF16),
         V((NY, J, K2), BF16), V((NY, J, idim), BF16),
         V((NY, K2), F32), V((NY, K2), F32), V((NY, 128), F32), V((2, NY * J, nk), BF16),
         V((NZ * NY, 128), F32),

time: 69.7 us -> 69 us (0.990)
  Pallas kernels: 68.9 us -> 68.2 us
where the time goes in v9:
time: 69 us; the launch traced here: 68.8 us
  Pallas kernels  68.2 us (99%)
    pallas_call x1, Pallas kernels, body(): pl.pallas_call(functools.partial(kernel, dims, keys / 32.0), out_shape=sh...  66.3 us
    pallas_call x1, Pallas kernels, body(): pl.pallas_call(store, out_shape=shapes, in_specs=[vm] * 3, out_specs=tupl...  1.93 us

profile of v9, /device:TPU:1, one launch (start us, length us, event | category | flops | bytes accessed | tf_op | source)
XLA Modules:
  0.0 68.8 jit_solution(15434789585179742074)
XLA Ops:
  0.6 66.3 %indexer_backward.1 = (f32[2,8,128]{2,1,0:T(8,128)}, f32[2,8]{1,0:T(2,128)}, f32[1024,128]{1,0:T(8,128)}) custom-call(bf16[2,16,576]{2,1,0:T(8,128)(2,1)} %q_hbm.1, bf16[576,1024]{1,0:T(8,128)(2,1)} %bitcast.1, f32[2,16]{1,0:T(2,128)} %lse_hbm.1, bf16[2,8,128]{2,1,0:T(8,128)(2,1)} %qi_hbm.1, bf16[1024,128]{1,0:T(8,128)(2,1)} %k_hbm.1, f32[2,8]{1,0:T(2,128)} %w_hbm.1), custom_call_target="tpu_custom_call" | custom-call | tf_op jit(solution)/shard_map/indexer_backward/pallas_call | solution.py:420
  66.9 1.9 %store_results.1 = (f32[2,8,128]{2,1,0:T(8,128)}, f32[2,8]{1,0:T(2,128)}, f32[1024,128]{1,0:T(8,128)}) custom-call(f32[2,8,128]{2,1,0:T(8,128)} %get-tuple-element.6.a_ref, f32[2,8]{1,0:T(2,128)} %get-tuple-element.7.b_ref, f32[1024,128]{1,0:T(8,128)} %get-tuple-element.8.c_ref), custom_call_target="tpu_custom_call" | custom-call | tf_op jit(solution)/shard_map/store_results/pallas_call | solution.py:431
